TPU v7x, 32 devices: a whole 2x2x4 slice. The times are simulated.
32 devices in a mesh: dp: 4 (over z), gx: 2 (over y), gy: 4 (over x, core).
Axes of the slice: x: 2, y: 2, z: 4, core: 2. Of those that a mesh axis runs over, the one named last changes fastest.
Arguments:
- volume: bfloat16 [4, 64, 96, 4, 128], P('dp', 'gx', 'gy'), may hold values from -6 to 6
- cotangent: bfloat16 [4, 32, 48, 2, 128], P('dp', 'gx', 'gy'), may hold values from -6 to 6
- w_first: bfloat16 [27, 128, 128], replicated, may hold values from -0.109375 to 0.109375
- w_second: bfloat16 [27, 128, 128], replicated, may hold values from -0.109375 to 0.109375
Outputs:
- grad_volume: bfloat16 [4, 64, 96, 4, 128], P('dp', 'gx', 'gy')
- grad_first: float32 [27, 128, 128], P(None, ('gx', 'gy'))
- grad_second: float32 [27, 128, 128], P(None, ('gx', 'gy'))
All inputs are finite; a program needn't handle non-finite values.
Results may differ from a plain program's by a relative error of at most 0.0095.
Values may be sent and summed in bfloat16 or wider, within the bound.
A program may use at most 64 MiB of HBM per device.

v0:
```python
import jax
import jax.numpy as jnp
from jax import lax
from jax.sharding import PartitionSpec as P


def with_halo(cells, sides, width):
    for axis, dim in sides:
        count = lax.axis_size(axis)
        ends = count - 1
        head = lax.slice_in_dim(cells, 0, width, axis=dim)
        tail = lax.slice_in_dim(cells, cells.shape[dim] - width, cells.shape[dim], axis=dim)
        cells = jnp.concatenate(
            [
                lax.ppermute(tail, axis, [(i, (i + 1) % count) for i in range(ends)]),
                cells,
                lax.ppermute(head, axis, [((i + 1) % count, i) for i in range(ends)]),
            ],
            axis=dim,
        )
    return cells


def shifted(block, axis, distance):
    devices = range(lax.axis_size(axis))
    route = [(i - distance, i) for i in devices if i - distance in devices]
    return lax.ppermute(block, axis, route)


def convolve(values, kernel, pads, dilation):
    return lax.conv_general_dilated(
        values,
        kernel,
        (1, 1, 1),
        pads,
        lhs_dilation=(dilation, dilation, dilation),
        dimension_numbers=("NDHWC", "DHWIO", "NDHWC"),
        preferred_element_type=jnp.float32,
    )


def silu_slope(values):
    sigma = jax.nn.sigmoid(values)
    return sigma * (1.0 + values * (1.0 - sigma))


def weight_grad(values, grads, pads, dilation):
    result = lax.conv_general_dilated(
        values,
        grads,
        (1, 1, 1),
        pads,
        rhs_dilation=(dilation, dilation, dilation),
        dimension_numbers=("CDHWN", "IDHWO", "NDHWC"),
        preferred_element_type=jnp.float32,
    )
    result = result[:, :3, :3, :3]
    inputs = result.shape[0]
    outputs = result.shape[4]
    return jnp.transpose(result, (1, 2, 3, 0, 4)).reshape(27, inputs, outputs)


def local(volume, cotangent, w_first, w_second):
    channels = w_first.shape[1]
    kernel_one = w_first.reshape(3, 3, 3, channels, channels)
    kernel_two = w_second.reshape(3, 3, 3, channels, channels)
    flipped_one = jnp.swapaxes(kernel_one[::-1, ::-1, ::-1], 3, 4)
    flipped_two = jnp.swapaxes(kernel_two[::-1, ::-1, ::-1], 3, 4)
    slab_pad = ((0, 0), (0, 0), (1, 1))
    widened = with_halo(volume, (("gx", 1), ("gy", 2)), 1)
    preact = convolve(widened, kernel_one, slab_pad, 1)
    hidden = jax.nn.silu(preact).astype(jnp.bfloat16)
    edge_row = shifted(cotangent[:, :1], "gx", -1)
    extended = jnp.concatenate([cotangent, edge_row], 1)
    edge_col = shifted(extended[:, :, :1], "gy", -1)
    extended = jnp.concatenate([extended, edge_col], 2)
    grad_hidden = convolve(extended, flipped_two, ((1, 0), (1, 0), (1, 2)), 2)
    grad_pre = (grad_hidden * silu_slope(preact)).astype(jnp.bfloat16)
    grad_cycle = with_halo(grad_pre, (("gx", 1), ("gy", 2)), 1)
    grad_volume = convolve(grad_cycle, flipped_one, slab_pad, 1).astype(jnp.bfloat16)
    first_local = weight_grad(widened, grad_pre, ((0, 0), (0, 0), (1, 1)), 1)
    second_local = weight_grad(hidden, extended, ((1, 2), (1, 2), (1, 1)), 2)
    summed = (
        lax.psum(first_local.astype(jnp.bfloat16), "dp").astype(jnp.float32),
        lax.psum(second_local.astype(jnp.bfloat16), "dp").astype(jnp.float32),
    )
    shares = (
        lax.psum_scatter(summed[0], ("gx", "gy"), scatter_dimension=1, tiled=True),
        lax.psum_scatter(summed[1], ("gx", "gy"), scatter_dimension=1, tiled=True),
    )
    return (grad_volume, shares[0], shares[1])


def solution(mesh):
    return jax.shard_map(
        local,
        mesh=mesh,
        in_specs=(P("dp", "gx", "gy", None, None), P("dp", "gx", "gy", None, None), P(), P()),
        out_specs=(
            P("dp", "gx", "gy", None, None),
            P(None, ("gx", "gy"), None),
            P(None, ("gx", "gy"), None),
        ),
        check_vma=False,
    )
```

profile of v0, /device:TPU:0, one launch (start us, length us, event | category | flops | bytes accessed | tf_op | source)
XLA Modules:
  0.0 271.3 jit_solution(10999313578141423012)
XLA Ops:
  8.0 1.3 collective-permute-start
  10.1 4.9 %collective-permute-start.2 = (bf16[1,1,24,4,128]{4,0,3,2,1:T(2,128)(2,1)S(1)}, bf16[1,1,24,4,128]{4,0,3,2,1:T(2,128)(2,1)S(1)}, u32[]{:S(2)}, u32[]{:S(2)}) collective-permute-start(bf16[1,1,24,4,128]{4,0,3,2,1:T(2,128)(2,1)S(1)} %copy.15), channel_id=1, source_target_pairs={{0,4},{1,5},{2,6},{3,7},{8,12},{9,13},{10,14},{11,15},{16,20},{17,... | collective-permute-start | bytes 73736 | tf_op jit(solution)/shard_map/ppermute | solution.py:15
  15.1 1.3 collective-permute-start.3
  17.5 1.3 collective-permute-start.1
  18.9 2.9 %constant_dynamic-update-slice_fusion.3 = bf16[1,34,24,4,128]{4,0,3,2,1:T(2,128)(2,1)S(1)} fusion(bf16[1,34,24,4,128]{4,0,3,2,1:T(2,128)(2,1)S(1)} %constant_dynamic-update-slice_fusion.4, bf16[1,32,24,4,128]{4,3,2,1,0:T(4,128)(2,1)} %param.4), kind=kLoop, calls=%fused_computation.17 | loop fusion | bytes 2359296
  22.0 3.0 %collective-permute-start.4 = (bf16[1,34,1,4,128]{4,0,3,2,1:T(2,128)(2,1)S(1)}, bf16[1,34,1,4,128]{4,0,3,2,1:T(2,128)(2,1)S(1)}, u32[]{:S(2)}, u32[]{:S(2)}) collective-permute-start(bf16[1,34,1,4,128]{4,0,3,2,1:T(2,128)(2,1)S(1)} %get-tuple-element.10), channel_id=1, source_target_pairs={{0,1},{1,2},{2,3},{4,5},{5,6},{6,7},{8,9},{9,10},{10,11},{12,13},{... | collective-permute-start | bytes 104456 | tf_op jit(solution)/shard_map/ppermute | solution.py:15
  25.0 1.8 collective-permute-start.5
  27.2 2.8 %collective-permute-done.5 = bf16[1,34,1,4,128]{4,0,3,2,1:T(2,128)(2,1)S(1)} collective-permute-done((bf16[1,34,1,4,128]{4,0,3,2,1:T(2,128)(2,1)S(1)}, bf16[1,34,1,4,128]{4,0,3,2,1:T(2,128)(2,1)S(1)}, u32[]{:S(2)}, u32[]{:S(2)}) %collective-permute-start.5) | collective-permute-done | bytes 34848 | tf_op jit(solution)/shard_map/ppermute | solution.py:17
  29.9 2.7 %pad_maximum_fusion = bf16[1,34,26,4,128]{4,0,3,2,1:T(2,128)(2,1)S(1)} fusion(bf16[1,34,1,4,128]{4,0,3,2,1:T(2,128)(2,1)S(1)} %collective-permute-done.5, bf16[1,34,24,4,128]{4,0,3,2,1:T(2,128)(2,1)S(1)} %constant_dynamic-update-slice_fusion.2, bf16[1,34,1,4,128]{4,0,3,2,1:T(2,128)(2,1)S(1)} %collective-permute-done.4), kind=kLoop, calls=%fused_computation | loop fusion | flops 905216 | bytes 1810432 | tf_op jit(solution)/shard_map/concatenate | solution.py:13
  32.7 20.4 %add_divide_fusion = (f32[1,32,24,4,128]{4,0,3,2,1:T(1,128)S(1)}, f32[1,32,24,4,128]{4,0,3,2,1:T(1,128)S(1)}) fusion(bf16[1,34,26,4,128]{4,0,3,2,1:T(2,128)(2,1)S(1)} %pad_maximum_fusion, bf16[3,3,3,128,128]{4,3,2,1,0:T(8,128)(2,1)S(1)} %bitcast.12), kind=kOutput, calls=%fused_computation.5 | convolution fusion | flops 2266103808 | bytes 4935680 | tf_op jit(solution)/shard_map/conv_general_dilated | solution.py:31
  54.8 10.1 %multiply_convert_fusion.1 = bf16[1,32,24,4,128]{4,0,3,2,1:T(2,128)(2,1)S(1)} fusion(f32[1,32,24,4,128]{4,0,3,2,1:T(1,128)S(1)} %get-tuple-element.16, f32[1,32,24,4,128]{4,0,3,2,1:T(1,128)S(1)} %get-tuple-element.17, bf16[3,3,3,128,128]{4,3,2,1,0:T(8,128)(2,1)S(1)} %bitcast.16, bf16[1,17,13,2,128]{4,0,3,2,1:T(2,128)(2,1)S(1)} %pad_maximum_fusion.13), kind=kOutput, calls=%fused_computation.4 | convolution fusion | flops 285474816 | bytes 4930048 | tf_op jit(solution)/shard_map/conv_general_dilated | solution.py:31
  65.0 26.1 %convolution_convert_fusion = bf16[3,3,3,128,128]{4,3,2,1,0:T(8,128)(2,1)} fusion(bf16[1,34,26,4,128]{4,0,3,2,1:T(2,128)(2,1)S(1)} %pad_maximum_fusion, bf16[1,32,24,4,128]{4,0,3,2,1:T(2,128)(2,1)S(1)} %multiply_convert_fusion.1), kind=kOutput, calls=%fused_computation.8 | convolution fusion | flops 2265366528 | bytes 2576384 | tf_op jit(solution)/shard_map/transpose | solution.py:60
  91.1 7.0 %fusion.3 = bf16[3,3,3,128,128]{4,3,2,1,0:T(8,128)(2,1)} fusion(f32[1,32,24,4,128]{4,0,3,2,1:T(1,128)S(1)} %copy-done.12, f32[1,32,24,4,128]{4,0,3,2,1:T(1,128)S(1)} %copy-done.10, bf16[1,17,1,2,128]{4,0,3,2,1:T(2,128)(2,1)S(1)} %copy-done.7, bf16[1,17,12,2,128]{4,0,3,2,1:T(2,128)(2,1)S(1)} %copy-done.3), kind=kOutput, calls=%fused_computation.9 | convolution fusion | flops 284570624 | bytes 4143616 | tf_op jit(solution)/shard_map/transpose | solution.py:60
  98.1 80.0 %all-reduce.3.cloned.1.call-done = (bf16[27,128,128]{2,1,0:T(8,128)(2,1)}, bf16[27,128,128]{2,1,0:T(8,128)(2,1)}) async-done(((bf16[27,128,128]{2,1,0:T(8,128)(2,1)}, bf16[27,128,128]{2,1,0:T(8,128)(2,1)}), (bf16[27,128,128]{2,1,0:T(8,128)(2,1)}, bf16[27,128,128]{2,1,0:T(8,128)(2,1)})) %all-reduce.3.cloned.1.call-update) | async-done | bytes 1769488 | tf_op jit(solution)/shard_map/psum | solution.py:84
  178.2 2.6 convert_element_type.31
  180.9 3.5 %collective-permute-start.6 = (bf16[1,1,24,4,128]{4,0,3,2,1:T(2,128)(2,1)S(1)}, bf16[1,1,24,4,128]{4,0,3,2,1:T(2,128)(2,1)S(1)}, u32[]{:S(2)}, u32[]{:S(2)}) collective-permute-start(bf16[1,1,24,4,128]{4,0,3,2,1:T(2,128)(2,1)S(1)} %get-tuple-element.12), channel_id=1, source_target_pairs={{0,4},{1,5},{2,6},{3,7},{8,12},{9,13},{10,14},{11,15},{16,20},{17,... | collective-permute-start | bytes 73736 | tf_op jit(solution)/shard_map/ppermute | solution.py:15
  184.5 1.3 collective-permute-start.7
  186.2 4.3 %collective-permute-done.7 = bf16[1,1,24,4,128]{4,0,3,2,1:T(2,128)(2,1)S(1)} collective-permute-done((bf16[1,1,24,4,128]{4,0,3,2,1:T(2,128)(2,1)S(1)}, bf16[1,1,24,4,128]{4,0,3,2,1:T(2,128)(2,1)S(1)}, u32[]{:S(2)}, u32[]{:S(2)}) %collective-permute-start.7) | collective-permute-done | bytes 24608 | tf_op jit(solution)/shard_map/ppermute | solution.py:17
  190.7 1.9 collective-permute-start.8
  193.9 1.4 convert_element_type.35
  195.3 1.6 collective-permute-done.9
  197.0 20.4 %fusion.2 = bf16[1,32,24,4,128]{4,0,3,2,1:T(2,128)(2,1)S(1)} fusion(bf16[3,3,3,128,128]{4,3,2,1,0:T(8,128)(2,1)S(1)} %bitcast.13, bf16[1,34,1,4,128]{4,0,3,2,1:T(2,128)(2,1)} %collective-permute-done.9, bf16[1,1,24,4,128]{4,0,3,2,1:T(2,128)(2,1)S(1)} %copy-done.5, bf16[1,32,24,4,128]{4,0,3,2,1:T(2,128)(2,1)S(1)} %multiply_convert_fusion.1, ...), kind=kOutput, calls=%fused_computation.7 | convolution fusion | flops 2269843456 | bytes 2576384 | tf_op jit(solution)/shard_map/conv_general_dilated | solution.py:31
  218.5 2.4 reduce-scatter.3.cloned.1.call-done
  220.9 43.7 %reduce-scatter.5.cloned.1.call-done = f32[27,16,128]{2,1,0:T(8,128)} async-done(((f32[27,128,128]{2,1,0:T(8,128)}), f32[27,16,128]{2,1,0:T(8,128)}) %reduce-scatter.5.cloned.1.call-update) | async-done | bytes 221200 | tf_op jit(solution)/shard_map/reduce_scatter | solution.py:89
  (55 shorter events, 8.4 us)
Async XLA Ops:
  7.2 25.5 %copy-start = (bf16[27,128,128]{2,1,0:T(8,128)(2,1)S(1)}, bf16[27,128,128]{2,1,0:T(8,128)(2,1)}, u32[]{:S(2)}) copy-start(bf16[27,128,128]{2,1,0:T(8,128)(2,1)} %param.6) | copy-start | bytes 2654212
  7.2 171.0 %all-reduce.3.cloned.1.call-start = ((), (), s32[]{:S(2)}) async-start(), calls=%async_computation.4 | async-start | bytes 3538944 | tf_op jit(solution)/shard_map/psum | solution.py:84
  8.0 9.5 %collective-permute-start = (bf16[1,1,12,2,128]{4,0,3,2,1:T(2,128)(2,1)S(1)}, bf16[1,1,12,2,128]{4,0,3,2,1:T(2,128)(2,1)S(1)}, u32[]{:S(2)}, u32[]{:S(2)}) collective-permute-start(bf16[1,1,12,2,128]{4,0,3,2,1:T(2,128)(2,1)S(1)} %copy.17), channel_id=1, source_target_pairs={{4,0},{5,1},{6,2},{7,3},{12,8},{13,9},{14,10},{15,11},{20,16},{21,... | collective-permute-start | bytes 18440 | tf_op jit(solution)/shard_map/ppermute | solution.py:27
  10.1 8.7 %collective-permute-start.2 = (bf16[1,1,24,4,128]{4,0,3,2,1:T(2,128)(2,1)S(1)}, bf16[1,1,24,4,128]{4,0,3,2,1:T(2,128)(2,1)S(1)}, u32[]{:S(2)}, u32[]{:S(2)}) collective-permute-start(bf16[1,1,24,4,128]{4,0,3,2,1:T(2,128)(2,1)S(1)} %copy.15), channel_id=1, source_target_pairs={{0,4},{1,5},{2,6},{3,7},{8,12},{9,13},{10,14},{11,15},{16,20},{17,... | collective-permute-start | bytes 73736 | tf_op jit(solution)/shard_map/ppermute | solution.py:15
  15.1 6.7 %collective-permute-start.3 = (bf16[1,1,24,4,128]{4,0,3,2,1:T(2,128)(2,1)S(1)}, bf16[1,1,24,4,128]{4,0,3,2,1:T(2,128)(2,1)S(1)}, u32[]{:S(2)}, u32[]{:S(2)}) collective-permute-start(bf16[1,1,24,4,128]{4,0,3,2,1:T(2,128)(2,1)S(1)} %copy.16), channel_id=1, source_target_pairs={{4,0},{5,1},{6,2},{7,3},{12,8},{13,9},{14,10},{15,11},{20,16},{21,... | collective-permute-start | bytes 73736 | tf_op jit(solution)/shard_map/ppermute | solution.py:17
  17.5 15.2 %copy-start.2 = (bf16[1,17,12,2,128]{4,0,3,2,1:T(2,128)(2,1)}, bf16[1,17,12,2,128]{4,0,3,2,1:T(2,128)(2,1)S(1)}, u32[]{:S(2)}) copy-start(bf16[1,17,12,2,128]{4,0,3,2,1:T(2,128)(2,1)S(1)} %constant_dynamic-update-slice_fusion) | copy-start | bytes 313348
  17.5 9.3 %collective-permute-start.1 = (bf16[1,17,1,2,128]{4,0,3,2,1:T(2,128)(2,1)S(1)}, bf16[1,17,1,2,128]{4,0,3,2,1:T(2,128)(2,1)S(1)}, u32[]{:S(2)}, u32[]{:S(2)}) collective-permute-start(bf16[1,17,1,2,128]{4,0,3,2,1:T(2,128)(2,1)S(1)} %slice.42), channel_id=1, source_target_pairs={{1,0},{2,1},{3,2},{5,4},{6,5},{7,6},{9,8},{10,9},{11,10},{13,12},{... | collective-permute-start | bytes 26120 | tf_op jit(solution)/shard_map/ppermute | solution.py:27
  22.0 5.1 %collective-permute-start.4 = (bf16[1,34,1,4,128]{4,0,3,2,1:T(2,128)(2,1)S(1)}, bf16[1,34,1,4,128]{4,0,3,2,1:T(2,128)(2,1)S(1)}, u32[]{:S(2)}, u32[]{:S(2)}) collective-permute-start(bf16[1,34,1,4,128]{4,0,3,2,1:T(2,128)(2,1)S(1)} %get-tuple-element.10), channel_id=1, source_target_pairs={{0,1},{1,2},{2,3},{4,5},{5,6},{6,7},{8,9},{9,10},{10,11},{12,13},{... | collective-permute-start | bytes 104456 | tf_op jit(solution)/shard_map/ppermute | solution.py:15
  25.0 4.9 %collective-permute-start.5 = (bf16[1,34,1,4,128]{4,0,3,2,1:T(2,128)(2,1)S(1)}, bf16[1,34,1,4,128]{4,0,3,2,1:T(2,128)(2,1)S(1)}, u32[]{:S(2)}, u32[]{:S(2)}) collective-permute-start(bf16[1,34,1,4,128]{4,0,3,2,1:T(2,128)(2,1)S(1)} %get-tuple-element.11), channel_id=1, source_target_pairs={{1,0},{2,1},{3,2},{5,4},{6,5},{7,6},{9,8},{10,9},{11,10},{13,12},{... | collective-permute-start | bytes 104456 | tf_op jit(solution)/shard_map/ppermute | solution.py:17
  26.8 5.9 %copy-start.6 = (bf16[1,17,1,2,128]{4,0,3,2,1:T(2,128)(2,1)}, bf16[1,17,1,2,128]{4,0,3,2,1:T(2,128)(2,1)S(1)}, u32[]{:S(2)}) copy-start(bf16[1,17,1,2,128]{4,0,3,2,1:T(2,128)(2,1)S(1)} %collective-permute-done.1) | copy-start | bytes 26116
  32.7 22.1 %copy-start.8 = (bf16[27,128,128]{2,1,0:T(8,128)(2,1)S(1)}, bf16[27,128,128]{2,1,0:T(8,128)(2,1)}, u32[]{:S(2)}) copy-start(bf16[27,128,128]{2,1,0:T(8,128)(2,1)} %param.7) | copy-start | bytes 2654212
  65.0 26.1 %copy-start.3 = (bf16[1,17,12,2,128]{4,0,3,2,1:T(2,128)(2,1)S(1)}, bf16[1,17,12,2,128]{4,0,3,2,1:T(2,128)(2,1)}, u32[]{:S(2)}) copy-start(bf16[1,17,12,2,128]{4,0,3,2,1:T(2,128)(2,1)} %copy-done.2) | copy-start | bytes 313348
  65.0 26.1 %copy-start.7 = (bf16[1,17,1,2,128]{4,0,3,2,1:T(2,128)(2,1)S(1)}, bf16[1,17,1,2,128]{4,0,3,2,1:T(2,128)(2,1)}, u32[]{:S(2)}) copy-start(bf16[1,17,1,2,128]{4,0,3,2,1:T(2,128)(2,1)} %copy-done.6) | copy-start | bytes 26116
  65.0 26.1 %copy-start.10 = (f32[1,32,24,4,128]{4,0,3,2,1:T(1,128)S(1)}, f32[1,32,24,4,128]{4,0,3,2,1:T(1,128)}, u32[]{:S(2)}) copy-start(f32[1,32,24,4,128]{4,0,3,2,1:T(1,128)} %copy-done.9) | copy-start | bytes 4718596
  65.0 26.1 %copy-start.12 = (f32[1,32,24,4,128]{4,0,3,2,1:T(1,128)S(1)}, f32[1,32,24,4,128]{4,0,3,2,1:T(1,128)}, u32[]{:S(2)}) copy-start(f32[1,32,24,4,128]{4,0,3,2,1:T(1,128)} %copy-done.11) | copy-start | bytes 4718596
  98.1 122.9 %reduce-scatter.3.cloned.1.call-start = ((), (), s32[]{:S(2)}) async-start(), calls=%async_computation.2 | async-start | bytes 1990656 | tf_op jit(solution)/shard_map/reduce_scatter | solution.py:88
  180.8 13.1 %copy-start.1 = (bf16[27,128,128]{2,1,0:T(8,128)(2,1)S(1)}, bf16[27,128,128]{2,1,0:T(8,128)(2,1)}, u32[]{:S(2)}) copy-start(bf16[27,128,128]{2,1,0:T(8,128)(2,1)} %get-tuple-element.7) | copy-start | bytes 2654212
  180.8 83.8 %reduce-scatter.5.cloned.1.call-start = ((), (), s32[]{:S(2)}) async-start(), calls=%async_computation.3 | async-start | bytes 1990656 | tf_op jit(solution)/shard_map/reduce_scatter | solution.py:89
  180.9 5.3 %collective-permute-start.6 = (bf16[1,1,24,4,128]{4,0,3,2,1:T(2,128)(2,1)S(1)}, bf16[1,1,24,4,128]{4,0,3,2,1:T(2,128)(2,1)S(1)}, u32[]{:S(2)}, u32[]{:S(2)}) collective-permute-start(bf16[1,1,24,4,128]{4,0,3,2,1:T(2,128)(2,1)S(1)} %get-tuple-element.12), channel_id=1, source_target_pairs={{0,4},{1,5},{2,6},{3,7},{8,12},{9,13},{10,14},{11,15},{16,20},{17,... | collective-permute-start | bytes 73736 | tf_op jit(solution)/shard_map/ppermute | solution.py:15
  184.5 6.0 %collective-permute-start.7 = (bf16[1,1,24,4,128]{4,0,3,2,1:T(2,128)(2,1)S(1)}, bf16[1,1,24,4,128]{4,0,3,2,1:T(2,128)(2,1)S(1)}, u32[]{:S(2)}, u32[]{:S(2)}) collective-permute-start(bf16[1,1,24,4,128]{4,0,3,2,1:T(2,128)(2,1)S(1)} %get-tuple-element.13), channel_id=1, source_target_pairs={{4,0},{5,1},{6,2},{7,3},{12,8},{13,9},{14,10},{15,11},{20,16},{21,... | collective-permute-start | bytes 73736 | tf_op jit(solution)/shard_map/ppermute | solution.py:17
  190.5 3.4 %copy-start.4 = (bf16[1,1,24,4,128]{4,0,3,2,1:T(2,128)(2,1)}, bf16[1,1,24,4,128]{4,0,3,2,1:T(2,128)(2,1)S(1)}, u32[]{:S(2)}) copy-start(bf16[1,1,24,4,128]{4,0,3,2,1:T(2,128)(2,1)S(1)} %collective-permute-done.7) | copy-start | bytes 73732
  190.7 4.7 %collective-permute-start.8 = (bf16[1,34,1,4,128]{4,0,3,2,1:T(2,128)(2,1)S(1)}, bf16[1,34,1,4,128]{4,0,3,2,1:T(2,128)(2,1)}, u32[]{:S(2)}, u32[]{:S(2)}) collective-permute-start(bf16[1,34,1,4,128]{4,0,3,2,1:T(2,128)(2,1)S(1)} %get-tuple-element.8), channel_id=1, source_target_pairs={{0,1},{1,2},{2,3},{4,5},{5,6},{6,7},{8,9},{9,10},{10,11},{12,13},{... | collective-permute-start | bytes 104456 | tf_op jit(solution)/shard_map/ppermute | solution.py:15
  192.6 4.4 %collective-permute-start.9 = (bf16[1,34,1,4,128]{4,0,3,2,1:T(2,128)(2,1)S(1)}, bf16[1,34,1,4,128]{4,0,3,2,1:T(2,128)(2,1)}, u32[]{:S(2)}, u32[]{:S(2)}) collective-permute-start(bf16[1,34,1,4,128]{4,0,3,2,1:T(2,128)(2,1)S(1)} %get-tuple-element.9), channel_id=1, source_target_pairs={{1,0},{2,1},{3,2},{5,4},{6,5},{7,6},{9,8},{10,9},{11,10},{13,12},{... | collective-permute-start | bytes 104456 | tf_op jit(solution)/shard_map/ppermute | solution.py:17
  195.3 1.7 copy-start.5
  (2 other events, 2.8 us)
Sparse Core Ops, SparseCore 0:
  98.2 79.9 all-reduce.2
  182.5 38.4 reduce-scatter.2
  225.2 39.3 reduce-scatter.4
where the time goes:
time: 275 us; the launch traced here: 271 us
  waiting for transfers between devices  135 us (49%)
  matrix products  84 us (31%)
  starting transfers between devices  21.7 us (8%)
  between operations  14.3 us (5%)
  local copies, waits for them, and re-layouts  8.86 us (3%)
  other arithmetic  7.29 us (3%)
    psum x1, waiting for transfers between devices, local(): lax.psum(first_local.astype(jnp.bfloat16), 'dp').astype(jnp.float32)  80 us
    conv_general_dilated x3, matrix products, convolve(): lax.conv_general_dilated(values, kernel, (1, 1, 1), pads, lhs_dilation=(d...  51 us
    reduce_scatter x1, waiting for transfers between devices, local(): lax.psum_scatter(summed[1], ('gx', 'gy'), scatter_dimension=1, tiled=True)  43.7 us
    transpose x2, matrix products, weight_grad(): return jnp.transpose(result, (1, 2, 3, 0, 4)).reshape(27, inputs, outputs)  33 us
    ppermute x4, starting transfers between devices, with_halo(): lax.ppermute(tail, axis, [(i, (i + 1) % count) for i in range(ends)])  13.3 us
    ppermute x4, waiting for transfers between devices, with_halo(): lax.ppermute(head, axis, [((i + 1) % count, i) for i in range(ends)])  8.64 us
    unnamed x33, local copies, waits for them, and re-layouts  6.96 us
    ppermute x4, starting transfers between devices, with_halo(): lax.ppermute(head, axis, [((i + 1) % count, i) for i in range(ends)])  5.62 us
  transfers between devices with their start and end apart: 13, of which 7 were waited for; matrix products, arithmetic and copies ran while one was open for 11% of the time, Pallas kernels for 0%

commit v1 on v0

v1 whole, which is shorter than its diff:
```python
import jax
import jax.numpy as jnp
from jax import lax
from jax.experimental import pallas as pl
from jax.experimental.pallas import tpu as pltpu
from jax.sharding import PartitionSpec as P

BF = jnp.bfloat16
F32 = jnp.float32
NT = (((1,), (1,)), ((), ()))
PAIRS = (((1, 0),), ((0, 1), (2, 0)))


def wide(cells):
    gx, gy = lax.axis_size("gx"), lax.axis_size("gy")
    up = lambda a, n, v: lax.ppermute(v, a, [(i, i + 1) for i in range(n - 1)])
    down = lambda a, n, v: lax.ppermute(v, a, [(i + 1, i) for i in range(n - 1)])
    cells = jnp.concatenate([up("gy", gy, cells[:, -1:]), cells, down("gy", gy, cells[:, :1])], 1)
    even, odd = cells[0], cells[1]
    before = jnp.concatenate([up("gx", gx, odd[:, -1:]), odd[:, :-1]], 1)
    after = jnp.concatenate([even[:, 1:], down("gx", gx, even[:, :1])], 1)
    return jnp.stack([before, even, odd, after])


def coarse(cells):
    gx, gy = lax.axis_size("gx"), lax.axis_size("gy")
    down = lambda a, n, v: lax.ppermute(v, a, [(i + 1, i) for i in range(n - 1)])
    cells = jnp.concatenate([cells, down("gy", gy, cells[:1])], 0)
    following = jnp.concatenate([cells[:, 1:], down("gx", gx, cells[:, :1])], 1)
    return jnp.stack([cells, following])


def conv_dot(x_ref, w_ref, bands, px, half, transposed):
    ny, nm = x_ref.shape[1] - 2, x_ref.shape[2]
    c = w_ref.shape[1]
    lo = half * c
    parts = [
        x_ref[px + a, b : b + ny, :, lo : lo + 3 * c].reshape(ny * nm, 3 * c)
        for a in range(3)
        for b in range(3)
    ]
    lhs = jnp.concatenate(parts, 1)
    if transposed:
        return lax.dot_general(lhs, bands[half], NT, preferred_element_type=F32)
    return jnp.dot(lhs, bands[half], preferred_element_type=F32)


def fill_bands(w_ref, bands, transposed):
    c = w_ref.shape[1]
    zero = jnp.zeros((c, c), BF)
    for half in range(2):
        for s in range(9):
            for k in range(3):
                for o in range(2):
                    tap = (k + half) - (o + 2 * half) + 1
                    good = 0 <= tap <= 2
                    rows = slice((3 * s + k) * c, (3 * s + k + 1) * c)
                    cols = slice(o * c, (o + 1) * c)
                    if transposed:
                        bands[half, cols, rows] = w_ref[26 - 3 * s - tap] if good else zero
                    else:
                        bands[half, rows, cols] = w_ref[3 * s + tap] if good else zero


def grads_kernel(x_ref, c_ref, w1_ref, w2_ref, gp_ref, g1_ref, g2_ref, bands, pre, gh, hid_t, gp_t, hid):
    ny, nm = x_ref.shape[1] - 2, x_ref.shape[2]
    nj = ny // 2
    c = w1_ref.shape[1]
    fill_bands(w1_ref, bands, False)
    for px in range(2):
        for half in range(2):
            pre[px, :, 2 * half * c : 2 * (half + 1) * c] = conv_dot(x_ref, w1_ref, bands, px, half, False)
    zero = jnp.zeros((c, c), BF)
    for px in range(2):
        for py in range(2):
            total = None
            for a, ci in PAIRS[px]:
                for b, dj in PAIRS[py]:
                    w = lambda t: w2_ref[9 * a + 3 * b + t]
                    left = jnp.concatenate([w(1), w(2), zero, zero], 0)
                    right = jnp.concatenate([zero, w(0), w(1), w(2)], 0)
                    rhs = jnp.concatenate([left, right], 1)
                    lhs = c_ref[ci, dj : dj + nj].reshape(nj * nm, 2 * c)
                    term = lax.dot_general(lhs, rhs, NT, preferred_element_type=F32)
                    total = term if total is None else total + term
            gh[px, :, py] = total.reshape(nj, nm, 4 * c)

    for px in range(2):
        def cells(j, _):
            for py in range(2):
                y = 2 * j + py
                v = pre[px, pl.ds(pl.multiple_of(y * nm, nm), nm), :]
                sigma = jax.nn.sigmoid(v)
                hid[px, py, j] = (v * sigma).astype(BF)
                gp_ref[px, y] = (gh[px, j, py] * (sigma * (1.0 + v * (1.0 - sigma)))).astype(BF)
            return _

        lax.fori_loop(0, nj, cells, 0)
    for px in range(2):
        gp_t[:, px * ny * nm : (px + 1) * ny * nm] = gp_ref[px].reshape(ny * nm, 4 * c).T
        for py in range(2):
            hid_t[px, py] = hid[px, py].reshape(nj * nm, 4 * c).T
    for a in range(3):
        px = 0 if a == 1 else 1
        ci = 1 if a == 0 else 0
        for b in range(3):
            py = 0 if b == 1 else 1
            dj = 1 if b == 0 else 0
            rhs = c_ref[ci, dj : dj + nj].reshape(nj * nm, 2 * c)
            r = jnp.dot(hid_t[px, py], rhs, preferred_element_type=F32)
            blk = lambda z, k: r[z * c : (z + 1) * c, k * c : (k + 1) * c]
            t = 9 * a + 3 * b
            g2_ref[t] = blk(1, 1).astype(BF)
            g2_ref[t + 1] = (blk(0, 0) + blk(2, 1)).astype(BF)
            g2_ref[t + 2] = (blk(1, 0) + blk(3, 1)).astype(BF)
    for a in range(3):
        for b in range(3):
            sums = [None, None, None]
            for half in range(2):
                rhs = jnp.concatenate(
                    [
                        x_ref[px + a, b : b + ny, :, half * c : (half + 3) * c].reshape(ny * nm, 3 * c)
                        for px in range(2)
                    ],
                    0,
                )
                r = jnp.dot(gp_t[2 * half * c : 2 * (half + 1) * c, :], rhs, preferred_element_type=F32)
                for o in range(2):
                    for k in range(3):
                        tap = (k + half) - (o + 2 * half) + 1
                        if 0 <= tap <= 2:
                            term = r[o * c : (o + 1) * c, k * c : (k + 1) * c]
                            sums[tap] = term if sums[tap] is None else sums[tap] + term
            for tap in range(3):
                g1_ref[9 * a + 3 * b + tap] = sums[tap].T.astype(BF)


def volume_kernel(x_ref, w_ref, out_ref, bands):
    ny, nm = x_ref.shape[1] - 2, x_ref.shape[2]
    c = w_ref.shape[1]
    fill_bands(w_ref, bands, True)
    for px in range(2):
        for half in range(2):
            r = conv_dot(x_ref, w_ref, bands, px, half, True)
            out_ref[px, :, :, 2 * half * c : 2 * (half + 1) * c] = r.reshape(ny, nm, 2 * c).astype(BF)


VMEM = pl.BlockSpec(memory_space=pltpu.VMEM)
PARAMS = pltpu.CompilerParams(vmem_limit_bytes=48 * 1024 * 1024)


def local(volume, cotangent, w_first, w_second):
    _, nx, ny, nz, c = volume.shape
    nm, nj, lanes = nx // 2, ny // 2, nz * c
    split = volume.reshape(nm, 2, ny, lanes).transpose(1, 2, 0, 3)
    cells = wide(split)
    grads = coarse(cotangent.reshape(nm, nj, 2 * c).transpose(1, 0, 2))
    weight = jax.ShapeDtypeStruct((27, c, c), BF)
    grad_pre, first, second = pl.pallas_call(
        grads_kernel,
        out_shape=(jax.ShapeDtypeStruct((2, ny, nm, lanes), BF), weight, weight),
        in_specs=[VMEM] * 4,
        out_specs=(VMEM,) * 3,
        scratch_shapes=[
            pltpu.VMEM((2, 27 * c, 2 * c), BF),
            pltpu.VMEM((2, ny * nm, lanes), F32),
            pltpu.VMEM((2, nj, 2, nm, lanes), F32),
            pltpu.VMEM((2, 2, lanes, nj * nm), BF),
            pltpu.VMEM((lanes, 2 * ny * nm), BF),
            pltpu.VMEM((2, 2, nj, nm, lanes), BF),
        ],
        compiler_params=PARAMS,
    )(cells, grads, w_first, w_second)
    both = jnp.stack([first, second])
    share = lax.psum_scatter(both, ("gx", "gy"), scatter_dimension=2, tiled=True)
    share = lax.psum(share, "dp").astype(F32)
    out = pl.pallas_call(
        volume_kernel,
        out_shape=jax.ShapeDtypeStruct((2, ny, nm, lanes), BF),
        in_specs=[VMEM] * 2,
        out_specs=VMEM,
        scratch_shapes=[pltpu.VMEM((2, 2 * c, 27 * c), BF)],
        compiler_params=PARAMS,
    )(wide(grad_pre), w_first)
    grad_volume = out.transpose(2, 0, 1, 3).reshape(1, nx, ny, nz, c)
    return (grad_volume, share[0], share[1])


def solution(mesh):
    return jax.shard_map(
        local,
        mesh=mesh,
        in_specs=(P("dp", "gx", "gy", None, None), P("dp", "gx", "gy", None, None), P(), P()),
        out_specs=(
            P("dp", "gx", "gy", None, None),
            P(None, ("gx", "gy"), None),
            P(None, ("gx", "gy"), None),
        ),
        check_vma=False,
    )
```

time: 275 us -> 136 us (0.49); the launches traced: 271 us -> 135 us
  matrix products: 84 us -> 0 us
  waiting for transfers between devices: 135 us -> 72.8 us
  Pallas kernels: 0 us -> 13.9 us
    conv_general_dilated x3 -> x0, matrix products: 51 us -> none  [convolve(): lax.conv_general_dilated(values, kernel, (1, 1, 1), pads, lhs_dilation=(d...]
    psum x1, waiting for transfers between devices: 80 us -> 32.3 us  [local(): share = lax.psum(share, 'dp').astype(F32)]
    transpose x2 -> x0, matrix products: 33 us -> none  [weight_grad(): return jnp.transpose(result, (1, 2, 3, 0, 4)).reshape(27, inputs, outputs)]
    reduce_scatter x2 -> x1, waiting for transfers between devices: 46.1 us -> 29 us  [local(): lax.psum_scatter(both, ('gx', 'gy'), scatter_dimension=2, tiled=True)]
    pallas_call x0 -> x2, Pallas kernels: none -> 13.9 us  [the longest x1 10.8 us: local(): pl.pallas_call(grads_kernel, out_shape=(jax.ShapeDtypeStruct((2, ny, nm,...]
    unnamed x33 -> x7, local copies, waits for them, and re-layouts: 6.96 us -> 1.59 us
    another operation x0 -> x10, other arithmetic: none -> 3.74 us  [the longest x6 2.26 us: wide(): return jnp.stack([before, even, odd, after])]
    reshape x0 -> x4, local copies, waits for them, and re-layouts: none -> 3.22 us  [the longest x2 2.09 us: local(): split = volume.reshape(nm, 2, ny, lanes).transpose(1, 2, 0, 3)]
  transfers between devices with their start and end apart: 13 -> 12, of which waited for: 7 -> 5; matrix products, arithmetic and copies ran while one was open for 11% -> 4% of each run, Pallas kernels for 0% -> 2%
where the time goes in v1:
time: 136 us; the launch traced here: 135 us
  waiting for transfers between devices  72.8 us (54%)
  starting transfers between devices  22.6 us (17%)
  between operations  14.4 us (11%)
  Pallas kernels  13.9 us (10%)
  local copies, waits for them, and re-layouts  6.59 us (5%)
  other arithmetic  4.87 us (4%)
    psum x1, waiting for transfers between devices, local(): share = lax.psum(share, 'dp').astype(F32)  32.3 us
    reduce_scatter x1, waiting for transfers between devices, local(): lax.psum_scatter(both, ('gx', 'gy'), scatter_dimension=2, tiled=True)  29 us
    ppermute x4, starting transfers between devices, wide(): up = lambda a, n, v: lax.ppermute(v, a, [(i, i + 1) for i in range(n - 1)])  14.7 us
    pallas_call x1, Pallas kernels, local(): pl.pallas_call(grads_kernel, out_shape=(jax.ShapeDtypeStruct((2, ny, nm,...  10.8 us
    ppermute x4, waiting for transfers between devices, wide(): lax.ppermute(v, a, [(i + 1, i) for i in range(n - 1)])  5.25 us
    ppermute x4, starting transfers between devices, wide(): lax.ppermute(v, a, [(i + 1, i) for i in range(n - 1)])  5.17 us
    ppermute x2, waiting for transfers between devices, coarse(): lax.ppermute(v, a, [(i + 1, i) for i in range(n - 1)])  4.57 us
    pallas_call x1, Pallas kernels, local(): pl.pallas_call(volume_kernel, out_shape=jax.ShapeDtypeStruct((2, ny, nm,...  3.15 us
  transfers between devices with their start and end apart: 12, of which 5 were waited for; matrix products, arithmetic and copies ran while one was open for 4% of the time, Pallas kernels for 2%

profile of v1, /device:TPU:0, one launch (start us, length us, event | category | flops | bytes accessed | tf_op | source)
XLA Modules:
  0.0 135.2 jit_solution(14820877557777050338)
XLA Ops:
  7.2 1.0 copy.9
  8.3 1.3 collective-permute-start.4
  9.6 1.7 %reshape.15 = bf16[16,2,24,512]{3,2,1,0:T(8,128)(2,1)S(1)} reshape(bf16[1,32,24,4,128]{4,3,2,1,0:T(4,128)(2,1)} %param.4) | data formatting | bytes 1572864 | tf_op jit(solution)/shard_map/reshape | solution.py:155
  11.7 3.0 %collective-permute-start = (bf16[2,1,16,512]{3,2,1,0:T(8,128)(2,1)S(1)}, bf16[2,1,16,512]{3,2,1,0:T(8,128)(2,1)S(1)}, u32[]{:S(2)}, u32[]{:S(2)}) collective-permute-start(bf16[2,1,16,512]{3,2,1,0:T(8,128)(2,1)S(1)} %get-tuple-element.15), channel_id=1, source_target_pairs={{0,1},{1,2},{2,3},{4,5},{5,6},{6,7},{8,9},{9,10},{10,11},{12,13},{... | collective-permute-start | bytes 98312 | tf_op jit(solution)/shard_map/ppermute | solution.py:16
  14.7 1.3 collective-permute-start.1
  16.1 1.3 collective-permute-start.5
  17.4 4.6 %collective-permute-done.5 = bf16[13,1,256]{2,1,0:T(2,128)(2,1)S(1)} collective-permute-done((bf16[13,1,256]{2,1,0:T(2,128)(2,1)S(1)}, bf16[13,1,256]{2,1,0:T(2,128)(2,1)S(1)}, u32[]{:S(2)}, u32[]{:S(2)}) %collective-permute-start.5) | collective-permute-done | bytes 6688 | tf_op jit(solution)/shard_map/ppermute | solution.py:27
  22.3 1.3 collective-permute-start.3
  23.8 4.5 %collective-permute-start.2 = (bf16[26,1,512]{2,1,0:T(2,128)(2,1)S(1)}, bf16[26,1,512]{2,1,0:T(2,128)(2,1)S(1)}, u32[]{:S(2)}, u32[]{:S(2)}) collective-permute-start(bf16[26,1,512]{2,1,0:T(2,128)(2,1)S(1)} %slice.89), channel_id=1, source_target_pairs={{0,4},{1,5},{2,6},{3,7},{8,12},{9,13},{10,14},{11,15},{16,20},{17,... | collective-permute-start | bytes 79880 | tf_op jit(solution)/shard_map/ppermute | solution.py:16
  28.5 1.7 %collective-permute-done.2 = bf16[26,1,512]{2,1,0:T(2,128)(2,1)S(1)} collective-permute-done((bf16[26,1,512]{2,1,0:T(2,128)(2,1)S(1)}, bf16[26,1,512]{2,1,0:T(2,128)(2,1)S(1)}, u32[]{:S(2)}, u32[]{:S(2)}) %collective-permute-start.2) | collective-permute-done | bytes 26656 | tf_op jit(solution)/shard_map/ppermute | solution.py:16
  30.4 1.5 %pad_maximum_fusion.1.x_ref = bf16[4,26,16,512]{3,2,1,0:T(8,128)(2,1)} fusion(bf16[1,26,16,512]{3,2,1,0:T(8,128)(2,1)S(1)} %maximum_bitcast_fusion.1, bf16[2,1,16,512]{3,2,1,0:T(8,128)(2,1)S(1)} %collective-permute-done.1, bf16[2,24,16,512]{3,2,1,0:T(8,128)(2,1)S(1)} %bitcast.42, bf16[2,1,16,512]{3,2,1,0:T(8,128)(2,1)S(1)} %collective-permute-done, ...), kind=kLoop, calls=%fused_computation.1 | loop fusion | flops 3407872 | bytes 3407872 | tf_op jit(solution)/shard_map/stack | solution.py:22
  32.4 10.8 %shard_map.67 = (bf16[2,24,16,512]{3,2,1,0:T(8,128)(2,1)S(1)}, bf16[27,128,128]{2,1,0:T(8,128)(2,1)S(1)}, bf16[27,128,128]{2,1,0:T(8,128)(2,1)S(1)}) custom-call(bf16[4,26,16,512]{3,2,1,0:T(8,128)(2,1)} %pad_maximum_fusion.1.x_ref, bf16[2,13,16,256]{3,2,1,0:T(8,128)(2,1)S(1)} %pad_maximum_fusion.4.c_ref, bf16[27,128,128]{2,1,0:T(8,128)(2,1)S(1)} %copy-done, ...), custom_call_target="tpu_custom_call" | custom-call | tf_op jit(solution)/shard_map/pallas_call | solution.py:159
  43.2 1.4 %pad_maximum_fusion = bf16[2,27,128,128]{3,2,1,0:T(8,128)(2,1)} fusion(bf16[1,27,128,128]{3,2,1,0:T(8,128)(2,1)S(1)} %bitcast.39, bf16[1,27,128,128]{3,2,1,0:T(8,128)(2,1)S(1)} %bitcast.38), kind=kLoop, calls=%fused_computation | loop fusion | flops 884736 | bytes 3538944 | tf_op jit(solution)/shard_map/stack | solution.py:174
  44.7 2.4 %collective-permute-start.6 = (bf16[2,1,16,512]{3,2,1,0:T(8,128)(2,1)S(1)}, bf16[2,1,16,512]{3,2,1,0:T(8,128)(2,1)S(1)}, u32[]{:S(2)}, u32[]{:S(2)}) collective-permute-start(bf16[2,1,16,512]{3,2,1,0:T(8,128)(2,1)S(1)} %get-tuple-element.14), channel_id=1, source_target_pairs={{0,1},{1,2},{2,3},{4,5},{5,6},{6,7},{8,9},{9,10},{10,11},{12,13},{... | collective-permute-start | bytes 98312 | tf_op jit(solution)/shard_map/ppermute | solution.py:16
  47.1 1.3 collective-permute-start.7
  48.5 5.2 %collective-permute-done.7 = bf16[2,1,16,512]{3,2,1,0:T(8,128)(2,1)S(1)} collective-permute-done((bf16[2,1,16,512]{3,2,1,0:T(8,128)(2,1)S(1)}, bf16[2,1,16,512]{3,2,1,0:T(8,128)(2,1)S(1)}, u32[]{:S(2)}, u32[]{:S(2)}) %collective-permute-start.7) | collective-permute-done | bytes 32800 | tf_op jit(solution)/shard_map/ppermute | solution.py:17
  53.9 1.3 collective-permute-start.9
  55.3 4.7 %collective-permute-start.8 = (bf16[26,1,512]{2,1,0:T(2,128)(2,1)S(1)}, bf16[26,1,512]{2,1,0:T(2,128)(2,1)S(1)}, u32[]{:S(2)}, u32[]{:S(2)}) collective-permute-start(bf16[26,1,512]{2,1,0:T(2,128)(2,1)S(1)} %slice.100), channel_id=1, source_target_pairs={{0,4},{1,5},{2,6},{3,7},{8,12},{9,13},{10,14},{11,15},{16,20},{17,... | collective-permute-start | bytes 79880 | tf_op jit(solution)/shard_map/ppermute | solution.py:16
  60.2 29.0 %reduce-scatter.2.cloned.1.call-done = bf16[2,27,16,128]{3,2,1,0:T(8,128)(2,1)} async-done(((bf16[2,27,128,128]{3,2,1,0:T(8,128)(2,1)}), bf16[2,27,16,128]{3,2,1,0:T(8,128)(2,1)}) %reduce-scatter.2.cloned.1.call-update) | async-done | bytes 221200 | tf_op jit(solution)/shard_map/reduce_scatter | solution.py:175
  89.6 3.2 %shard_map.68 = bf16[2,24,16,512]{3,2,1,0:T(8,128)(2,1)S(1)} custom-call(bf16[4,26,16,512]{3,2,1,0:T(8,128)(2,1)S(1)} %pad_maximum_fusion.2.x_ref, bf16[27,128,128]{2,1,0:T(8,128)(2,1)S(1)} %copy-done), custom_call_target="tpu_custom_call" | custom-call | tf_op jit(solution)/shard_map/pallas_call | solution.py:177
  93.2 1.1 reshape.17
  94.3 32.3 %all-reduce.2.cloned.1.call-done = bf16[2,27,16,128]{3,2,1,0:T(8,128)(2,1)} async-done(((bf16[2,27,16,128]{3,2,1,0:T(8,128)(2,1)}), bf16[2,27,16,128]{3,2,1,0:T(8,128)(2,1)}) %all-reduce.2.cloned.1.call-update) | async-done | bytes 221200 | tf_op jit(solution)/shard_map/psum | solution.py:176
  126.6 1.0 convert_element_type.3
  127.6 0.8 slice_bitcast_fusion.4
  (43 shorter events, 3.3 us)
Async XLA Ops:
  7.2 82.0 %reduce-scatter.2.cloned.1.call-start = ((), (), s32[]{:S(2)}) async-start(), calls=%async_computation.1 | async-start | bytes 1990656 | tf_op jit(solution)/shard_map/reduce_scatter | solution.py:175
  8.3 7.8 %collective-permute-start.4 = (bf16[1,16,256]{2,1,0:T(8,128)(2,1)S(1)}, bf16[1,16,256]{2,1,0:T(8,128)(2,1)S(1)}, u32[]{:S(2)}, u32[]{:S(2)}) collective-permute-start(bf16[1,16,256]{2,1,0:T(8,128)(2,1)S(1)} %slice.94), channel_id=1, source_target_pairs={{1,0},{2,1},{3,2},{5,4},{6,5},{7,6},{9,8},{10,9},{11,10},{13,12},{... | collective-permute-start | bytes 24584 | tf_op jit(solution)/shard_map/ppermute | solution.py:27
  11.7 10.3 %collective-permute-start = (bf16[2,1,16,512]{3,2,1,0:T(8,128)(2,1)S(1)}, bf16[2,1,16,512]{3,2,1,0:T(8,128)(2,1)S(1)}, u32[]{:S(2)}, u32[]{:S(2)}) collective-permute-start(bf16[2,1,16,512]{3,2,1,0:T(8,128)(2,1)S(1)} %get-tuple-element.15), channel_id=1, source_target_pairs={{0,1},{1,2},{2,3},{4,5},{5,6},{6,7},{8,9},{9,10},{10,11},{12,13},{... | collective-permute-start | bytes 98312 | tf_op jit(solution)/shard_map/ppermute | solution.py:16
  14.7 7.3 %collective-permute-start.1 = (bf16[2,1,16,512]{3,2,1,0:T(8,128)(2,1)S(1)}, bf16[2,1,16,512]{3,2,1,0:T(8,128)(2,1)S(1)}, u32[]{:S(2)}, u32[]{:S(2)}) collective-permute-start(bf16[2,1,16,512]{3,2,1,0:T(8,128)(2,1)S(1)} %get-tuple-element.16), channel_id=1, source_target_pairs={{1,0},{2,1},{3,2},{5,4},{6,5},{7,6},{9,8},{10,9},{11,10},{13,12},{... | collective-permute-start | bytes 98312 | tf_op jit(solution)/shard_map/ppermute | solution.py:17
  16.1 5.9 %collective-permute-start.5 = (bf16[13,1,256]{2,1,0:T(2,128)(2,1)S(1)}, bf16[13,1,256]{2,1,0:T(2,128)(2,1)S(1)}, u32[]{:S(2)}, u32[]{:S(2)}) collective-permute-start(bf16[13,1,256]{2,1,0:T(2,128)(2,1)S(1)} %fusion.2), channel_id=1, source_target_pairs={{4,0},{5,1},{6,2},{7,3},{12,8},{13,9},{14,10},{15,11},{20,16},{21,... | collective-permute-start | bytes 19976 | tf_op jit(solution)/shard_map/ppermute | solution.py:27
  22.3 6.1 %collective-permute-start.3 = (bf16[26,1,512]{2,1,0:T(2,128)(2,1)S(1)}, bf16[26,1,512]{2,1,0:T(2,128)(2,1)S(1)}, u32[]{:S(2)}, u32[]{:S(2)}) collective-permute-start(bf16[26,1,512]{2,1,0:T(2,128)(2,1)S(1)} %slice.93), channel_id=1, source_target_pairs={{4,0},{5,1},{6,2},{7,3},{12,8},{13,9},{14,10},{15,11},{20,16},{21,... | collective-permute-start | bytes 79880 | tf_op jit(solution)/shard_map/ppermute | solution.py:17
  23.8 6.4 %collective-permute-start.2 = (bf16[26,1,512]{2,1,0:T(2,128)(2,1)S(1)}, bf16[26,1,512]{2,1,0:T(2,128)(2,1)S(1)}, u32[]{:S(2)}, u32[]{:S(2)}) collective-permute-start(bf16[26,1,512]{2,1,0:T(2,128)(2,1)S(1)} %slice.89), channel_id=1, source_target_pairs={{0,4},{1,5},{2,6},{3,7},{8,12},{9,13},{10,14},{11,15},{16,20},{17,... | collective-permute-start | bytes 79880 | tf_op jit(solution)/shard_map/ppermute | solution.py:16
  30.3 1.5 %copy-start = (bf16[27,128,128]{2,1,0:T(8,128)(2,1)S(1)}, bf16[27,128,128]{2,1,0:T(8,128)(2,1)}, u32[]{:S(2)}) copy-start(bf16[27,128,128]{2,1,0:T(8,128)(2,1)} %w_ref.1) | copy-start | bytes 2654212
  30.4 2.0 %copy-start.1 = (bf16[27,128,128]{2,1,0:T(8,128)(2,1)S(1)}, bf16[27,128,128]{2,1,0:T(8,128)(2,1)}, u32[]{:S(2)}) copy-start(bf16[27,128,128]{2,1,0:T(8,128)(2,1)} %w2_ref.1) | copy-start | bytes 2654212
  44.6 82.0 %all-reduce.2.cloned.1.call-start = ((), (), s32[]{:S(2)}) async-start(), calls=%async_computation.2 | async-start | bytes 442368 | tf_op jit(solution)/shard_map/psum | solution.py:176
  44.7 3.7 %collective-permute-start.6 = (bf16[2,1,16,512]{3,2,1,0:T(8,128)(2,1)S(1)}, bf16[2,1,16,512]{3,2,1,0:T(8,128)(2,1)S(1)}, u32[]{:S(2)}, u32[]{:S(2)}) collective-permute-start(bf16[2,1,16,512]{3,2,1,0:T(8,128)(2,1)S(1)} %get-tuple-element.14), channel_id=1, source_target_pairs={{0,1},{1,2},{2,3},{4,5},{5,6},{6,7},{8,9},{9,10},{10,11},{12,13},{... | collective-permute-start | bytes 98312 | tf_op jit(solution)/shard_map/ppermute | solution.py:16
  47.1 6.6 %collective-permute-start.7 = (bf16[2,1,16,512]{3,2,1,0:T(8,128)(2,1)S(1)}, bf16[2,1,16,512]{3,2,1,0:T(8,128)(2,1)S(1)}, u32[]{:S(2)}, u32[]{:S(2)}) collective-permute-start(bf16[2,1,16,512]{3,2,1,0:T(8,128)(2,1)S(1)} %get-tuple-element.13), channel_id=1, source_target_pairs={{1,0},{2,1},{3,2},{5,4},{6,5},{7,6},{9,8},{10,9},{11,10},{13,12},{... | collective-permute-start | bytes 98312 | tf_op jit(solution)/shard_map/ppermute | solution.py:17
  53.9 6.2 %collective-permute-start.9 = (bf16[26,1,512]{2,1,0:T(2,128)(2,1)S(1)}, bf16[26,1,512]{2,1,0:T(2,128)(2,1)S(1)}, u32[]{:S(2)}, u32[]{:S(2)}) collective-permute-start(bf16[26,1,512]{2,1,0:T(2,128)(2,1)S(1)} %slice.104), channel_id=1, source_target_pairs={{4,0},{5,1},{6,2},{7,3},{12,8},{13,9},{14,10},{15,11},{20,16},{21,... | collective-permute-start | bytes 79880 | tf_op jit(solution)/shard_map/ppermute | solution.py:17
  55.3 33.9 %collective-permute-start.8 = (bf16[26,1,512]{2,1,0:T(2,128)(2,1)S(1)}, bf16[26,1,512]{2,1,0:T(2,128)(2,1)S(1)}, u32[]{:S(2)}, u32[]{:S(2)}) collective-permute-start(bf16[26,1,512]{2,1,0:T(2,128)(2,1)S(1)} %slice.100), channel_id=1, source_target_pairs={{0,4},{1,5},{2,6},{3,7},{8,12},{9,13},{10,14},{11,15},{16,20},{17,... | collective-permute-start | bytes 79880 | tf_op jit(solution)/shard_map/ppermute | solution.py:16
Sparse Core Ops, SparseCore 0:
  44.7 44.4 reduce-scatter.1
  91.6 34.9 all-reduce.1

commit v2 on v1

--- a/solution.py
+++ b/solution.py
@@ -1,3 +1,5 @@
+import functools
+
 import jax
 import jax.numpy as jnp
 from jax import lax
@@ -149,6 +151,102 @@
 PARAMS = pltpu.CompilerParams(vmem_limit_bytes=48 * 1024 * 1024)
 
 
+def plane_orders(gx, gy):
+    gys = [("gy", 1 << k) for k in range(gy.bit_length() - 1)]
+    gxs = [("gx", 1 << k) for k in range(gx.bit_length() - 1)]
+    return (gys + gxs, gys[:1] + gxs + gys[1:])
+
+
+def by_halves(grad, order, gx, gy):
+    taps, c, _ = grad.shape
+    bits = [("gx", 1 << k) for k in reversed(range(gx.bit_length() - 1))]
+    bits += [("gy", 1 << k) for k in reversed(range(gy.bit_length() - 1))]
+    share = c // (gx * gy)
+    parts = grad.reshape((taps,) + (2,) * len(bits) + (share, c))
+    n = len(bits)
+    parts = parts.transpose(tuple(1 + bits.index(o) for o in order) + (0, n + 1, n + 2))
+    return parts.reshape(gx * gy, taps * share, c)
+
+
+def reduce_kernel(orders, dps, first_ref, second_ref, out1_ref, out2_ref, *scratch):
+    steps = len(orders[0]) + len(dps)
+    lands, sums = scratch[:steps], scratch[steps : 2 * steps - 1]
+    send_sem, recv_sem = scratch[-2:]
+    outs = (out1_ref, out2_ref)
+
+    def side(axis, bit):
+        at = lax.axis_index(axis)
+        mine = (at // bit) % 2
+        return mine, {axis: at + bit * (1 - 2 * mine)}
+
+    barrier = pltpu.get_barrier_semaphore()
+    for axis, bit in orders[0] + dps:
+        pl.semaphore_signal(
+            barrier, inc=1, device_id=side(axis, bit)[1], device_id_type=pl.DeviceIdType.MESH
+        )
+    pl.semaphore_wait(barrier, steps)
+
+    held = [first_ref, second_ref]
+    halving = len(orders[0])
+    plans = [orders[0] + dps, orders[1] + dps[::-1]]
+    for k in range(steps):
+        copies = []
+        for s in range(2):
+            mine, partner = side(*plans[s][k])
+            size = lands[k].shape[1]
+            src = held[s].at[pl.ds((1 - mine) * size, size)] if k < halving else held[s]
+            copy = pltpu.make_async_remote_copy(
+                src_ref=src,
+                dst_ref=lands[k].at[s],
+                send_sem=send_sem.at[k, s],
+                recv_sem=recv_sem.at[k, s],
+                device_id=partner,
+                device_id_type=pl.DeviceIdType.MESH,
+            )
+            copy.start()
+            copies.append(copy)
+        following = []
+        for s in range(2):
+            copies[s].wait()
+            mine, _ = side(*plans[s][k])
+            size = lands[k].shape[1]
+            target = outs[s] if k == steps - 1 else sums[k].at[s]
+            base = mine * size if k < halving else 0
+
+            def add(i, _):
+                total = held[s][base + i].astype(F32) + lands[k][s, i].astype(F32)
+                target[i] = total.astype(target.dtype)
+                return _
+
+            lax.fori_loop(0, size, add, 0)
+            following.append(target)
+        held = following
+
+
+def reduce_grads(first, second):
+    gx, gy, dp = (lax.axis_size(a) for a in ("gx", "gy", "dp"))
+    orders = plane_orders(gx, gy)
+    dps = [("dp", 1 << k) for k in range(dp.bit_length() - 1)]
+    taps, c, _ = first.shape
+    share = c // (gx * gy)
+    rows = taps * share
+    sizes = [gx * gy >> (k + 1) for k in range(len(orders[0]))] + [1] * len(dps)
+    out = jax.ShapeDtypeStruct((1, rows, c), F32)
+    one, two = pl.pallas_call(
+        functools.partial(reduce_kernel, orders, dps),
+        out_shape=(out, out),
+        in_specs=[VMEM] * 2,
+        out_specs=(VMEM,) * 2,
+        scratch_shapes=[pltpu.VMEM((2, n, rows, c), BF) for n in sizes]
+        + [pltpu.VMEM((2, n, rows, c), BF) for n in sizes[:-1]]
+        + [pltpu.SemaphoreType.DMA((len(sizes), 2)), pltpu.SemaphoreType.DMA((len(sizes), 2))],
+        compiler_params=pltpu.CompilerParams(
+            collective_id=0, has_side_effects=True, vmem_limit_bytes=48 * 1024 * 1024
+        ),
+    )(by_halves(first, orders[0], gx, gy), by_halves(second, orders[1], gx, gy))
+    return one.reshape(taps, share, c), two.reshape(taps, share, c)
+
+
 def local(volume, cotangent, w_first, w_second):
     _, nx, ny, nz, c = volume.shape
     nm, nj, lanes = nx // 2, ny // 2, nz * c
@@ -171,9 +269,7 @@
         ],
         compiler_params=PARAMS,
     )(cells, grads, w_first, w_second)
-    both = jnp.stack([first, second])
-    share = lax.psum_scatter(both, ("gx", "gy"), scatter_dimension=2, tiled=True)
-    share = lax.psum(share, "dp").astype(F32)
+    share = reduce_grads(first, second)
     out = pl.pallas_call(
         volume_kernel,
         out_shape=jax.ShapeDtypeStruct((2, ny, nm, lanes), BF),

time: 136 us -> 90.1 us (0.66)
  waiting for transfers between devices: 72.8 us -> 13 us
  Pallas kernels: 13.9 us -> 44.6 us
  between operations: 14.4 us -> 1 us
  other arithmetic: 4.87 us -> 2.46 us
  starting transfers between devices: 22.6 us -> 21.1 us
    psum x1 -> x0, waiting for transfers between devices: 32.3 us -> none  [local(): share = lax.psum(share, 'dp').astype(F32)]
    pallas_call x0 -> x1, Pallas kernels: none -> 30.7 us  [reduce_grads(): pl.pallas_call(functools.partial(reduce_kernel, orders, dps), out_shape=(...]
    reduce_scatter x1 -> x0, waiting for transfers between devices: 29 us -> none  [local(): lax.psum_scatter(both, ('gx', 'gy'), scatter_dimension=2, tiled=True)]
    ppermute x4, waiting for transfers between devices: 1.69 us -> 3.15 us  [wide(): up = lambda a, n, v: lax.ppermute(v, a, [(i, i + 1) for i in range(n - 1)])]
    another operation x1 -> x0, other arithmetic: 1.41 us -> none  [local(): both = jnp.stack([first, second])]
    ppermute x4, starting transfers between devices: 14.7 us -> 13.3 us  [wide(): up = lambda a, n, v: lax.ppermute(v, a, [(i, i + 1) for i in range(n - 1)])]
    unnamed x7 -> x9, local copies, waits for them, and re-layouts: 1.59 us -> 2.97 us
  transfers between devices with their start and end apart: 12 -> 10, of which waited for: 5 -> 4; matrix products, arithmetic and copies ran while one was open for 4% -> 4% of each run, Pallas kernels for 2% -> 34%
where the time goes in v2:
time: 90.1 us; the launch traced here: 89.7 us
  Pallas kernels  44.6 us (50%)
  starting transfers between devices  21.1 us (23%)
  waiting for transfers between devices  13 us (14%)
  local copies, waits for them, and re-layouts  7.49 us (8%)
  other arithmetic  2.46 us (3%)
  between operations  1 us (1%)
    pallas_call x1, Pallas kernels, reduce_grads(): pl.pallas_call(functools.partial(reduce_kernel, orders, dps), out_shape=(...  30.7 us
    ppermute x4, starting transfers between devices, wide(): up = lambda a, n, v: lax.ppermute(v, a, [(i, i + 1) for i in range(n - 1)])  13.3 us
    pallas_call x1, Pallas kernels, local(): pl.pallas_call(grads_kernel, out_shape=(jax.ShapeDtypeStruct((2, ny, nm,...  10.8 us
    ppermute x4, waiting for transfers between devices, wide(): lax.ppermute(v, a, [(i + 1, i) for i in range(n - 1)])  5.25 us
    ppermute x4, starting transfers between devices, wide(): lax.ppermute(v, a, [(i + 1, i) for i in range(n - 1)])  5.17 us
    ppermute x2, waiting for transfers between devices, coarse(): lax.ppermute(v, a, [(i + 1, i) for i in range(n - 1)])  4.57 us
    pallas_call x1, Pallas kernels, local(): pl.pallas_call(volume_kernel, out_shape=jax.ShapeDtypeStruct((2, ny, nm,...  3.15 us
    ppermute x4, waiting for transfers between devices, wide(): up = lambda a, n, v: lax.ppermute(v, a, [(i, i + 1) for i in range(n - 1)])  3.15 us
  transfers between devices with their start and end apart: 10, of which 4 were waited for; matrix products, arithmetic and copies ran while one was open for 4% of the time, Pallas kernels for 34%

profile of v2, /device:TPU:0, one launch (start us, length us, event | category | flops | bytes accessed | tf_op | source)
XLA Modules:
  0.0 89.7 jit_solution(10228694006175154587)
XLA Ops:
  0.6 1.0 %copy.11 = bf16[1,16,12,2,128]{4,3,1,2,0:T(2,128)(2,1)S(1)} copy(bf16[1,16,12,2,128]{4,3,2,1,0:T(2,128)(2,1)} %param.5) | data formatting | bytes 196608 | tf_op args[1]
  1.7 1.3 %collective-permute-start.4 = (bf16[1,16,256]{2,1,0:T(8,128)(2,1)S(1)}, bf16[1,16,256]{2,1,0:T(8,128)(2,1)S(1)}, u32[]{:S(2)}, u32[]{:S(2)}) collective-permute-start(bf16[1,16,256]{2,1,0:T(8,128)(2,1)S(1)} %slice.86), channel_id=1, source_target_pairs={{1,0},{2,1},{3,2},{5,4},{6,5},{7,6},{9,8},{10,9},{11,10},{13,12},{... | collective-permute-start | bytes 24584 | tf_op jit(solution)/shard_map/ppermute | solution.py:29
  3.0 1.7 %reshape.33 = bf16[16,2,24,512]{3,2,1,0:T(8,128)(2,1)S(1)} reshape(bf16[1,32,24,4,128]{4,3,2,1,0:T(4,128)(2,1)} %param.4) | data formatting | bytes 1572864 | tf_op jit(solution)/shard_map/reshape | solution.py:253
  5.1 3.0 %collective-permute-start = (bf16[2,1,16,512]{3,2,1,0:T(8,128)(2,1)S(1)}, bf16[2,1,16,512]{3,2,1,0:T(8,128)(2,1)S(1)}, u32[]{:S(2)}, u32[]{:S(2)}) collective-permute-start(bf16[2,1,16,512]{3,2,1,0:T(8,128)(2,1)S(1)} %get-tuple-element.19), channel_id=1, source_target_pairs={{0,1},{1,2},{2,3},{4,5},{5,6},{6,7},{8,9},{9,10},{10,11},{12,13},{... | collective-permute-start | bytes 98312 | tf_op jit(solution)/shard_map/ppermute | solution.py:18
  8.1 1.3 %collective-permute-start.1 = (bf16[2,1,16,512]{3,2,1,0:T(8,128)(2,1)S(1)}, bf16[2,1,16,512]{3,2,1,0:T(8,128)(2,1)S(1)}, u32[]{:S(2)}, u32[]{:S(2)}) collective-permute-start(bf16[2,1,16,512]{3,2,1,0:T(8,128)(2,1)S(1)} %get-tuple-element.20), channel_id=1, source_target_pairs={{1,0},{2,1},{3,2},{5,4},{6,5},{7,6},{9,8},{10,9},{11,10},{13,12},{... | collective-permute-start | bytes 98312 | tf_op jit(solution)/shard_map/ppermute | solution.py:19
  9.5 1.3 %collective-permute-start.5 = (bf16[13,1,256]{2,1,0:T(2,128)(2,1)S(1)}, bf16[13,1,256]{2,1,0:T(2,128)(2,1)S(1)}, u32[]{:S(2)}, u32[]{:S(2)}) collective-permute-start(bf16[13,1,256]{2,1,0:T(2,128)(2,1)S(1)} %fusion.2), channel_id=1, source_target_pairs={{4,0},{5,1},{6,2},{7,3},{12,8},{13,9},{14,10},{15,11},{20,16},{21,... | collective-permute-start | bytes 19976 | tf_op jit(solution)/shard_map/ppermute | solution.py:29
  10.8 4.6 %collective-permute-done.5 = bf16[13,1,256]{2,1,0:T(2,128)(2,1)S(1)} collective-permute-done((bf16[13,1,256]{2,1,0:T(2,128)(2,1)S(1)}, bf16[13,1,256]{2,1,0:T(2,128)(2,1)S(1)}, u32[]{:S(2)}, u32[]{:S(2)}) %collective-permute-start.5) | collective-permute-done | bytes 6688 | tf_op jit(solution)/shard_map/ppermute | solution.py:29
  15.7 1.3 %collective-permute-start.3 = (bf16[26,1,512]{2,1,0:T(2,128)(2,1)S(1)}, bf16[26,1,512]{2,1,0:T(2,128)(2,1)S(1)}, u32[]{:S(2)}, u32[]{:S(2)}) collective-permute-start(bf16[26,1,512]{2,1,0:T(2,128)(2,1)S(1)} %slice.85), channel_id=1, source_target_pairs={{4,0},{5,1},{6,2},{7,3},{12,8},{13,9},{14,10},{15,11},{20,16},{21,... | collective-permute-start | bytes 79880 | tf_op jit(solution)/shard_map/ppermute | solution.py:19
  17.2 4.5 %collective-permute-start.2 = (bf16[26,1,512]{2,1,0:T(2,128)(2,1)S(1)}, bf16[26,1,512]{2,1,0:T(2,128)(2,1)S(1)}, u32[]{:S(2)}, u32[]{:S(2)}) collective-permute-start(bf16[26,1,512]{2,1,0:T(2,128)(2,1)S(1)} %slice.81), channel_id=1, source_target_pairs={{0,4},{1,5},{2,6},{3,7},{8,12},{9,13},{10,14},{11,15},{16,20},{17,... | collective-permute-start | bytes 79880 | tf_op jit(solution)/shard_map/ppermute | solution.py:18
  21.9 1.7 %collective-permute-done.2 = bf16[26,1,512]{2,1,0:T(2,128)(2,1)S(1)} collective-permute-done((bf16[26,1,512]{2,1,0:T(2,128)(2,1)S(1)}, bf16[26,1,512]{2,1,0:T(2,128)(2,1)S(1)}, u32[]{:S(2)}, u32[]{:S(2)}) %collective-permute-start.2) | collective-permute-done | bytes 26656 | tf_op jit(solution)/shard_map/ppermute | solution.py:18
  23.8 1.5 %pad_maximum_fusion.x_ref = bf16[4,26,16,512]{3,2,1,0:T(8,128)(2,1)} fusion(bf16[1,26,16,512]{3,2,1,0:T(8,128)(2,1)S(1)} %maximum_bitcast_fusion.1, bf16[2,1,16,512]{3,2,1,0:T(8,128)(2,1)S(1)} %collective-permute-done.1, bf16[2,24,16,512]{3,2,1,0:T(8,128)(2,1)S(1)} %bitcast.50, bf16[2,1,16,512]{3,2,1,0:T(8,128)(2,1)S(1)} %collective-permute-done, ...), kind=kLoop, calls=%fused_computation | loop fusion | flops 3407872 | bytes 3407872 | tf_op jit(solution)/shard_map/stack | solution.py:24
  25.2 0.6 copy-done.1
  25.8 10.8 %shard_map.67 = (bf16[2,24,16,512]{3,2,1,0:T(8,128)(2,1)S(1)}, bf16[27,128,128]{2,1,0:T(8,128)(2,1)S(1)}, bf16[27,128,128]{2,1,0:T(8,128)(2,1)S(1)}) custom-call(bf16[4,26,16,512]{3,2,1,0:T(8,128)(2,1)} %pad_maximum_fusion.x_ref, bf16[2,13,16,256]{3,2,1,0:T(8,128)(2,1)S(1)} %pad_maximum_fusion.3.c_ref, bf16[27,128,128]{2,1,0:T(8,128)(2,1)S(1)} %copy-done, ...), custom_call_target="tpu_custom_call" | custom-call | tf_op jit(solution)/shard_map/pallas_call | solution.py:257
  36.6 2.4 %collective-permute-start.6 = (bf16[2,1,16,512]{3,2,1,0:T(8,128)(2,1)S(1)}, bf16[2,1,16,512]{3,2,1,0:T(8,128)(2,1)S(1)}, u32[]{:S(2)}, u32[]{:S(2)}) collective-permute-start(bf16[2,1,16,512]{3,2,1,0:T(8,128)(2,1)S(1)} %get-tuple-element.18), channel_id=1, source_target_pairs={{0,1},{1,2},{2,3},{4,5},{5,6},{6,7},{8,9},{9,10},{10,11},{12,13},{... | collective-permute-start | bytes 98312 | tf_op jit(solution)/shard_map/ppermute | solution.py:18
  39.1 1.3 %collective-permute-start.7 = (bf16[2,1,16,512]{3,2,1,0:T(8,128)(2,1)S(1)}, bf16[2,1,16,512]{3,2,1,0:T(8,128)(2,1)S(1)}, u32[]{:S(2)}, u32[]{:S(2)}) collective-permute-start(bf16[2,1,16,512]{3,2,1,0:T(8,128)(2,1)S(1)} %get-tuple-element.17), channel_id=1, source_target_pairs={{1,0},{2,1},{3,2},{5,4},{6,5},{7,6},{9,8},{10,9},{11,10},{13,12},{... | collective-permute-start | bytes 98312 | tf_op jit(solution)/shard_map/ppermute | solution.py:19
  40.4 5.2 %collective-permute-done.7 = bf16[2,1,16,512]{3,2,1,0:T(8,128)(2,1)S(1)} collective-permute-done((bf16[2,1,16,512]{3,2,1,0:T(8,128)(2,1)S(1)}, bf16[2,1,16,512]{3,2,1,0:T(8,128)(2,1)S(1)}, u32[]{:S(2)}, u32[]{:S(2)}) %collective-permute-start.7) | collective-permute-done | bytes 32800 | tf_op jit(solution)/shard_map/ppermute | solution.py:19
  45.8 1.3 %collective-permute-start.9 = (bf16[26,1,512]{2,1,0:T(2,128)(2,1)S(1)}, bf16[26,1,512]{2,1,0:T(2,128)(2,1)S(1)}, u32[]{:S(2)}, u32[]{:S(2)}) collective-permute-start(bf16[26,1,512]{2,1,0:T(2,128)(2,1)S(1)} %slice.96), channel_id=1, source_target_pairs={{4,0},{5,1},{6,2},{7,3},{12,8},{13,9},{14,10},{15,11},{20,16},{21,... | collective-permute-start | bytes 79880 | tf_op jit(solution)/shard_map/ppermute | solution.py:19
  47.4 30.7 %shard_map.69 = (f32[1,432,128]{2,1,0:T(8,128)S(1)}, f32[1,432,128]{2,1,0:T(8,128)S(1)}) custom-call(bf16[8,432,128]{2,1,0:T(8,128)(2,1)S(1)} %bitcast.41, bf16[8,432,128]{2,1,0:T(8,128)(2,1)S(1)} %bitcast.42), custom_call_target="tpu_custom_call" | custom-call | tf_op jit(solution)/shard_map/pallas_call | solution.py:235
  78.3 3.3 %collective-permute-start.8 = (bf16[26,1,512]{2,1,0:T(2,128)(2,1)S(1)}, bf16[26,1,512]{2,1,0:T(2,128)(2,1)S(1)}, u32[]{:S(2)}, u32[]{:S(2)}) collective-permute-start(bf16[26,1,512]{2,1,0:T(2,128)(2,1)S(1)} %slice.92), channel_id=1, source_target_pairs={{0,4},{1,5},{2,6},{3,7},{8,12},{9,13},{10,14},{11,15},{16,20},{17,... | collective-permute-start | bytes 79880 | tf_op jit(solution)/shard_map/ppermute | solution.py:18
  81.8 1.5 %collective-permute-done.8 = bf16[26,1,512]{2,1,0:T(2,128)(2,1)S(1)} collective-permute-done((bf16[26,1,512]{2,1,0:T(2,128)(2,1)S(1)}, bf16[26,1,512]{2,1,0:T(2,128)(2,1)S(1)}, u32[]{:S(2)}, u32[]{:S(2)}) %collective-permute-start.8) | collective-permute-done | bytes 26656 | tf_op jit(solution)/shard_map/ppermute | solution.py:18
  83.6 3.1 %shard_map.68 = bf16[2,24,16,512]{3,2,1,0:T(8,128)(2,1)S(1)} custom-call(bf16[4,26,16,512]{3,2,1,0:T(8,128)(2,1)S(1)} %pad_maximum_fusion.1.x_ref, bf16[27,128,128]{2,1,0:T(8,128)(2,1)S(1)} %copy-done), custom_call_target="tpu_custom_call" | custom-call | tf_op jit(solution)/shard_map/pallas_call | solution.py:273
  87.2 1.1 %reshape.35 = bf16[1,32,24,4,128]{4,3,2,1,0:T(4,128)(2,1)} reshape(bf16[16,2,24,512]{3,2,1,0:T(8,128)(2,1)S(1)} %copy.12) | data formatting | bytes 1572864 | tf_op jit(solution)/shard_map/reshape | solution.py:281
  88.3 0.7 copy.21
  89.0 0.7 copy.22
  (39 shorter events, 2.9 us)
Async XLA Ops:
  1.7 7.8 %collective-permute-start.4 = (bf16[1,16,256]{2,1,0:T(8,128)(2,1)S(1)}, bf16[1,16,256]{2,1,0:T(8,128)(2,1)S(1)}, u32[]{:S(2)}, u32[]{:S(2)}) collective-permute-start(bf16[1,16,256]{2,1,0:T(8,128)(2,1)S(1)} %slice.86), channel_id=1, source_target_pairs={{1,0},{2,1},{3,2},{5,4},{6,5},{7,6},{9,8},{10,9},{11,10},{13,12},{... | collective-permute-start | bytes 24584 | tf_op jit(solution)/shard_map/ppermute | solution.py:29
  5.1 10.3 %collective-permute-start = (bf16[2,1,16,512]{3,2,1,0:T(8,128)(2,1)S(1)}, bf16[2,1,16,512]{3,2,1,0:T(8,128)(2,1)S(1)}, u32[]{:S(2)}, u32[]{:S(2)}) collective-permute-start(bf16[2,1,16,512]{3,2,1,0:T(8,128)(2,1)S(1)} %get-tuple-element.19), channel_id=1, source_target_pairs={{0,1},{1,2},{2,3},{4,5},{5,6},{6,7},{8,9},{9,10},{10,11},{12,13},{... | collective-permute-start | bytes 98312 | tf_op jit(solution)/shard_map/ppermute | solution.py:18
  8.1 7.3 %collective-permute-start.1 = (bf16[2,1,16,512]{3,2,1,0:T(8,128)(2,1)S(1)}, bf16[2,1,16,512]{3,2,1,0:T(8,128)(2,1)S(1)}, u32[]{:S(2)}, u32[]{:S(2)}) collective-permute-start(bf16[2,1,16,512]{3,2,1,0:T(8,128)(2,1)S(1)} %get-tuple-element.20), channel_id=1, source_target_pairs={{1,0},{2,1},{3,2},{5,4},{6,5},{7,6},{9,8},{10,9},{11,10},{13,12},{... | collective-permute-start | bytes 98312 | tf_op jit(solution)/shard_map/ppermute | solution.py:19
  9.5 5.9 %collective-permute-start.5 = (bf16[13,1,256]{2,1,0:T(2,128)(2,1)S(1)}, bf16[13,1,256]{2,1,0:T(2,128)(2,1)S(1)}, u32[]{:S(2)}, u32[]{:S(2)}) collective-permute-start(bf16[13,1,256]{2,1,0:T(2,128)(2,1)S(1)} %fusion.2), channel_id=1, source_target_pairs={{4,0},{5,1},{6,2},{7,3},{12,8},{13,9},{14,10},{15,11},{20,16},{21,... | collective-permute-start | bytes 19976 | tf_op jit(solution)/shard_map/ppermute | solution.py:29
  15.7 6.1 %collective-permute-start.3 = (bf16[26,1,512]{2,1,0:T(2,128)(2,1)S(1)}, bf16[26,1,512]{2,1,0:T(2,128)(2,1)S(1)}, u32[]{:S(2)}, u32[]{:S(2)}) collective-permute-start(bf16[26,1,512]{2,1,0:T(2,128)(2,1)S(1)} %slice.85), channel_id=1, source_target_pairs={{4,0},{5,1},{6,2},{7,3},{12,8},{13,9},{14,10},{15,11},{20,16},{21,... | collective-permute-start | bytes 79880 | tf_op jit(solution)/shard_map/ppermute | solution.py:19
  17.2 6.4 %collective-permute-start.2 = (bf16[26,1,512]{2,1,0:T(2,128)(2,1)S(1)}, bf16[26,1,512]{2,1,0:T(2,128)(2,1)S(1)}, u32[]{:S(2)}, u32[]{:S(2)}) collective-permute-start(bf16[26,1,512]{2,1,0:T(2,128)(2,1)S(1)} %slice.81), channel_id=1, source_target_pairs={{0,4},{1,5},{2,6},{3,7},{8,12},{9,13},{10,14},{11,15},{16,20},{17,... | collective-permute-start | bytes 79880 | tf_op jit(solution)/shard_map/ppermute | solution.py:18
  23.8 1.5 %copy-start = (bf16[27,128,128]{2,1,0:T(8,128)(2,1)S(1)}, bf16[27,128,128]{2,1,0:T(8,128)(2,1)}, u32[]{:S(2)}) copy-start(bf16[27,128,128]{2,1,0:T(8,128)(2,1)} %w_ref.1) | copy-start | bytes 2654212
  23.8 2.0 %copy-start.1 = (bf16[27,128,128]{2,1,0:T(8,128)(2,1)S(1)}, bf16[27,128,128]{2,1,0:T(8,128)(2,1)}, u32[]{:S(2)}) copy-start(bf16[27,128,128]{2,1,0:T(8,128)(2,1)} %w2_ref.1) | copy-start | bytes 2654212
  36.6 3.8 %collective-permute-start.6 = (bf16[2,1,16,512]{3,2,1,0:T(8,128)(2,1)S(1)}, bf16[2,1,16,512]{3,2,1,0:T(8,128)(2,1)S(1)}, u32[]{:S(2)}, u32[]{:S(2)}) collective-permute-start(bf16[2,1,16,512]{3,2,1,0:T(8,128)(2,1)S(1)} %get-tuple-element.18), channel_id=1, source_target_pairs={{0,1},{1,2},{2,3},{4,5},{5,6},{6,7},{8,9},{9,10},{10,11},{12,13},{... | collective-permute-start | bytes 98312 | tf_op jit(solution)/shard_map/ppermute | solution.py:18
  39.1 6.6 %collective-permute-start.7 = (bf16[2,1,16,512]{3,2,1,0:T(8,128)(2,1)S(1)}, bf16[2,1,16,512]{3,2,1,0:T(8,128)(2,1)S(1)}, u32[]{:S(2)}, u32[]{:S(2)}) collective-permute-start(bf16[2,1,16,512]{3,2,1,0:T(8,128)(2,1)S(1)} %get-tuple-element.17), channel_id=1, source_target_pairs={{1,0},{2,1},{3,2},{5,4},{6,5},{7,6},{9,8},{10,9},{11,10},{13,12},{... | collective-permute-start | bytes 98312 | tf_op jit(solution)/shard_map/ppermute | solution.py:19
  45.8 35.9 %collective-permute-start.9 = (bf16[26,1,512]{2,1,0:T(2,128)(2,1)S(1)}, bf16[26,1,512]{2,1,0:T(2,128)(2,1)S(1)}, u32[]{:S(2)}, u32[]{:S(2)}) collective-permute-start(bf16[26,1,512]{2,1,0:T(2,128)(2,1)S(1)} %slice.96), channel_id=1, source_target_pairs={{4,0},{5,1},{6,2},{7,3},{12,8},{13,9},{14,10},{15,11},{20,16},{21,... | collective-permute-start | bytes 79880 | tf_op jit(solution)/shard_map/ppermute | solution.py:19
  78.3 4.9 %collective-permute-start.8 = (bf16[26,1,512]{2,1,0:T(2,128)(2,1)S(1)}, bf16[26,1,512]{2,1,0:T(2,128)(2,1)S(1)}, u32[]{:S(2)}, u32[]{:S(2)}) collective-permute-start(bf16[26,1,512]{2,1,0:T(2,128)(2,1)S(1)} %slice.92), channel_id=1, source_target_pairs={{0,4},{1,5},{2,6},{3,7},{8,12},{9,13},{10,14},{11,15},{16,20},{17,... | collective-permute-start | bytes 79880 | tf_op jit(solution)/shard_map/ppermute | solution.py:18

commit v3 on v2

--- a/solution.py
+++ b/solution.py
@@ -9,27 +9,106 @@
 
 BF = jnp.bfloat16
 F32 = jnp.float32
+VMEM = pl.BlockSpec(memory_space=pltpu.VMEM)
 NT = (((1,), (1,)), ((), ()))
 PAIRS = (((1, 0),), ((0, 1), (2, 0)))
 
 
-def wide(cells):
+TURNS = [(dx, dy) for dx in (1, -1, 0) for dy in (1, -1, 0)][:8]
+
+
+def swap_kernel(ys_ref, xs_ref, land_ref, send_sem, recv_sem):
     gx, gy = lax.axis_size("gx"), lax.axis_size("gy")
-    up = lambda a, n, v: lax.ppermute(v, a, [(i, i + 1) for i in range(n - 1)])
-    down = lambda a, n, v: lax.ppermute(v, a, [(i + 1, i) for i in range(n - 1)])
-    cells = jnp.concatenate([up("gy", gy, cells[:, -1:]), cells, down("gy", gy, cells[:, :1])], 1)
+    x, y = lax.axis_index("gx"), lax.axis_index("gy")
+    partners = [{"gx": (x + dx + gx) % gx, "gy": (y + dy + gy) % gy} for dx, dy in TURNS]
+    barrier = pltpu.get_barrier_semaphore()
+    for partner in partners:
+        pl.semaphore_signal(barrier, inc=1, device_id=partner, device_id_type=pl.DeviceIdType.MESH)
+    pl.semaphore_wait(barrier, len(TURNS))
+    copies = []
+    for k, (dx, dy) in enumerate(TURNS):
+        src = ys_ref.at[(1 + dy) // 2] if dx == 0 else xs_ref.at[(1 + dx) // 2]
+        copy = pltpu.make_async_remote_copy(
+            src_ref=src,
+            dst_ref=land_ref.at[k],
+            send_sem=send_sem.at[k],
+            recv_sem=recv_sem.at[k],
+            device_id=partners[k],
+            device_id_type=pl.DeviceIdType.MESH,
+        )
+        copy.start()
+        copies.append(copy)
+    for copy in copies:
+        copy.wait()
+
+
+def swap(ys, xs, place):
+    land = pl.pallas_call(
+        swap_kernel,
+        out_shape=jax.ShapeDtypeStruct((8,) + ys.shape[1:], BF),
+        in_specs=[VMEM] * 2,
+        out_specs=VMEM,
+        scratch_shapes=[pltpu.SemaphoreType.DMA((8,)), pltpu.SemaphoreType.DMA((8,))],
+        compiler_params=pltpu.CompilerParams(collective_id=place, has_side_effects=True),
+    )(ys, xs)
+    out = {}
+    x, y = lax.axis_index("gx"), lax.axis_index("gy")
+    has_x = {0: True, 1: x > 0, -1: x < lax.axis_size("gx") - 1}
+    has_y = {0: True, 1: y > 0, -1: y < lax.axis_size("gy") - 1}
+    for k, (dx, dy) in enumerate(TURNS):
+        good = jnp.logical_and(has_x[dx], has_y[dy])
+        out[dx, dy] = jnp.where(good, land[k], jnp.zeros((), BF))
+    return out
+
+
+def padded(rows, count, lanes):
+    return jnp.pad(rows, ((0, count - rows.shape[0]), (0, lanes - rows.shape[1])))
+
+
+def edges(cells):
+    _, ny, nm, lanes = cells.shape
+    rows = -(-max(2 * nm, ny) // 16) * 16
+    ys = [padded(cells[:, y].reshape(2 * nm, lanes), rows, lanes) for y in (0, ny - 1)]
+    xs = [padded(row, rows, lanes) for row in (cells[0, :, 0], cells[1, :, nm - 1])]
+    return ys, xs
+
+
+def widened(cells, got):
+    _, ny, nm, lanes = cells.shape
+    layer = lambda dy: got[0, dy][: 2 * nm].reshape(2, 1, nm, lanes)
+    cells = jnp.concatenate([layer(1), cells, layer(-1)], 1)
+
+    def column(dx):
+        parts = [got[dx, 1][ny - 1 : ny], got[dx, 0][:ny], got[dx, -1][:1]]
+        return jnp.concatenate(parts, 0)[:, None]
+
     even, odd = cells[0], cells[1]
-    before = jnp.concatenate([up("gx", gx, odd[:, -1:]), odd[:, :-1]], 1)
-    after = jnp.concatenate([even[:, 1:], down("gx", gx, even[:, :1])], 1)
+    before = jnp.concatenate([column(1), odd[:, :-1]], 1)
+    after = jnp.concatenate([even[:, 1:], column(-1)], 1)
     return jnp.stack([before, even, odd, after])
 
 
-def coarse(cells):
-    gx, gy = lax.axis_size("gx"), lax.axis_size("gy")
-    down = lambda a, n, v: lax.ppermute(v, a, [(i + 1, i) for i in range(n - 1)])
-    cells = jnp.concatenate([cells, down("gy", gy, cells[:1])], 0)
-    following = jnp.concatenate([cells[:, 1:], down("gx", gx, cells[:, :1])], 1)
-    return jnp.stack([cells, following])
+def widened_both(cells, coarse):
+    lanes = cells.shape[3]
+    nj, ni, few = coarse.shape
+    ys, xs = edges(cells)
+    top = ys[0].shape[0]
+    more = -(-max(nj, ni) // 16) * 16
+    low = lambda rows: padded(rows, more, lanes)
+    blank = jnp.zeros((more, lanes), BF)
+    ys = jnp.stack([jnp.concatenate([ys[0], low(coarse[0])]), jnp.concatenate([ys[1], blank])])
+    xs = jnp.stack([jnp.concatenate([xs[0], low(coarse[:, 0])]), jnp.concatenate([xs[1], blank])])
+    got = swap(ys, xs, 1)
+    tail = lambda dx, dy, n: got[dx, dy][top : top + n, :few]
+    long = jnp.concatenate([coarse, tail(0, -1, ni)[None]], 0)
+    column = jnp.concatenate([tail(-1, 0, nj), tail(-1, -1, 1)], 0)[:, None]
+    following = jnp.concatenate([long[:, 1:], column], 1)
+    return widened(cells, got), jnp.stack([long, following])
+
+
+def widened_again(cells):
+    ys, xs = edges(cells)
+    return widened(cells, swap(jnp.stack(ys), jnp.stack(xs), 2))
 
 
 def conv_dot(x_ref, w_ref, bands, px, half, transposed):
@@ -147,7 +226,6 @@
             out_ref[px, :, :, 2 * half * c : 2 * (half + 1) * c] = r.reshape(ny, nm, 2 * c).astype(BF)
 
 
-VMEM = pl.BlockSpec(memory_space=pltpu.VMEM)
 PARAMS = pltpu.CompilerParams(vmem_limit_bytes=48 * 1024 * 1024)
 
 
@@ -251,8 +329,7 @@
     _, nx, ny, nz, c = volume.shape
     nm, nj, lanes = nx // 2, ny // 2, nz * c
     split = volume.reshape(nm, 2, ny, lanes).transpose(1, 2, 0, 3)
-    cells = wide(split)
-    grads = coarse(cotangent.reshape(nm, nj, 2 * c).transpose(1, 0, 2))
+    cells, grads = widened_both(split, cotangent.reshape(nm, nj, 2 * c).transpose(1, 0, 2))
     weight = jax.ShapeDtypeStruct((27, c, c), BF)
     grad_pre, first, second = pl.pallas_call(
         grads_kernel,
@@ -277,7 +354,7 @@
         out_specs=VMEM,
         scratch_shapes=[pltpu.VMEM((2, 2 * c, 27 * c), BF)],
         compiler_params=PARAMS,
-    )(wide(grad_pre), w_first)
+    )(widened_again(grad_pre), w_first)
     grad_volume = out.transpose(2, 0, 1, 3).reshape(1, nx, ny, nz, c)
     return (grad_volume, share[0], share[1])
 

time: 90.1 us -> 82.1 us (0.911)
  starting transfers between devices: 21.1 us -> 0 us
  Pallas kernels: 44.6 us -> 65.2 us
  waiting for transfers between devices: 13 us -> 0 us
  other arithmetic: 2.46 us -> 7.33 us
    pallas_call x0 -> x2, Pallas kernels: none -> 22.8 us  [swap(): pl.pallas_call(swap_kernel, out_shape=jax.ShapeDtypeStruct((8,) + ys.shap...]
    ppermute x10 -> x0, starting transfers between devices: 21.1 us -> none  [the longest x4 13.3 us: wide(): up = lambda a, n, v: lax.ppermute(v, a, [(i, i + 1) for i in range(n - 1)])]
    ppermute x10 -> x0, waiting for transfers between devices: 13 us -> none  [the longest x4 5.25 us: wide(): lax.ppermute(v, a, [(i + 1, i) for i in range(n - 1)])]
    another operation x9 -> x15, other arithmetic: 2.31 us -> 4.96 us  [the longest x6 2.3 us: widened(): return jnp.stack([before, even, odd, after])]
    pallas_call x1, Pallas kernels: 30.7 us -> 28.4 us  [reduce_grads(): pl.pallas_call(functools.partial(reduce_kernel, orders, dps), out_shape=(...]
    slice x0 -> x12, other arithmetic: none -> 2.02 us  [the longest x2 1.9 us: swap(): out[dx, dy] = jnp.where(good, land[k], jnp.zeros((), BF))]
  transfers between devices with their start and end apart: 10 -> 0, of which waited for: 4 -> 0; matrix products, arithmetic and copies ran while one was open for 4% -> 0% of each run, Pallas kernels for 34% -> 0%
where the time goes in v3:
time: 82.1 us; the launch traced here: 81.7 us
  Pallas kernels  65.2 us (79%)
  local copies, waits for them, and re-layouts  8.01 us (10%)
  other arithmetic  7.33 us (9%)
  between operations  1.16 us (1%)
    pallas_call x1, Pallas kernels, reduce_grads(): pl.pallas_call(functools.partial(reduce_kernel, orders, dps), out_shape=(...  28.4 us
    pallas_call x2, Pallas kernels, swap(): pl.pallas_call(swap_kernel, out_shape=jax.ShapeDtypeStruct((8,) + ys.shap...  22.8 us
    pallas_call x1, Pallas kernels, local(): pl.pallas_call(grads_kernel, out_shape=(jax.ShapeDtypeStruct((2, ny, nm,...  10.8 us
    pallas_call x1, Pallas kernels, local(): pl.pallas_call(volume_kernel, out_shape=jax.ShapeDtypeStruct((2, ny, nm,...  3.15 us
    unnamed x9, local copies, waits for them, and re-layouts  2.93 us
    another operation x6, other arithmetic, widened(): return jnp.stack([before, even, odd, after])  2.3 us
    reshape x2, local copies, waits for them, and re-layouts, local(): split = volume.reshape(nm, 2, ny, lanes).transpose(1, 2, 0, 3)  2.09 us
    slice x2, other arithmetic, swap(): out[dx, dy] = jnp.where(good, land[k], jnp.zeros((), BF))  1.9 us

profile of v3, /device:TPU:0, one launch (start us, length us, event | category | flops | bytes accessed | tf_op | source)
XLA Modules:
  0.0 81.7 jit_solution(7497741975317059048)
XLA Ops:
  0.7 1.0 %copy.36 = bf16[1,16,12,2,128]{4,3,1,2,0:T(2,128)(2,1)S(1)} copy(bf16[1,16,12,2,128]{4,3,2,1,0:T(2,128)(2,1)} %param.5) | data formatting | bytes 196608 | tf_op args[1]
  1.7 1.7 %reshape.127 = bf16[16,2,24,512]{3,2,1,0:T(8,128)(2,1)S(1)} reshape(bf16[1,32,24,4,128]{4,3,2,1,0:T(4,128)(2,1)} %param.4) | data formatting | bytes 1572864 | tf_op jit(solution)/shard_map/reshape | solution.py:331
  3.4 0.4 copy.56
  3.9 0.7 pad_maximum_fusion.6.ys_ref
  4.7 0.7 pad_maximum_fusion.7.xs_ref
  5.3 13.6 %shard_map.67 = bf16[8,48,512]{2,1,0:T(8,128)(2,1)} custom-call(bf16[2,48,512]{2,1,0:T(8,128)(2,1)} %pad_maximum_fusion.6.ys_ref, bf16[2,48,512]{2,1,0:T(8,128)(2,1)} %pad_maximum_fusion.7.xs_ref), custom_call_target="tpu_custom_call" | custom-call | tf_op jit(solution)/shard_map/pallas_call | solution.py:46
  18.9 1.0 %fusion.22 = (bf16[1,48,512]{2,1,0:T(8,128)(2,1)S(1)}, bf16[1,48,512]{2,1,0:T(8,128)(2,1)S(1)}, bf16[1,48,512]{2,1,0:T(8,128)(2,1)S(1)}, bf16[1,48,512]{2,1,0:T(...) fusion(bf16[8,48,512]{2,1,0:T(8,128)(2,1)} %shard_map.67, ...), kind=kLoop, calls=%fused_computation.79 | loop fusion | flops 73728 | bytes 786435 | tf_op jit(solution)/shard_map/slice | solution.py:60
  20.5 0.2 maximum_bitcast_fusion
  21.0 1.5 %pad_maximum_fusion.x_ref = bf16[4,26,16,512]{3,2,1,0:T(8,128)(2,1)} fusion(bf16[1,26,16,512]{3,2,1,0:T(8,128)(2,1)S(1)} %maximum_bitcast_fusion.1, bf16[2,1,16,512]{3,2,1,0:T(8,128)(2,1)S(1)} %bitcast.141, bf16[2,24,16,512]{3,2,1,0:T(8,128)(2,1)S(1)} %bitcast.127, bf16[2,1,16,512]{3,2,1,0:T(8,128)(2,1)S(1)} %bitcast.139, ...), kind=kLoop, calls=%fused_computation | loop fusion | flops 3407872 | bytes 3407872 | tf_op jit(solution)/shard_map/stack | solution.py:88
  22.5 0.6 copy-done.1
  23.0 10.8 %shard_map.68 = (bf16[2,24,16,512]{3,2,1,0:T(8,128)(2,1)S(1)}, bf16[27,128,128]{2,1,0:T(8,128)(2,1)S(1)}, bf16[27,128,128]{2,1,0:T(8,128)(2,1)S(1)}) custom-call(bf16[4,26,16,512]{3,2,1,0:T(8,128)(2,1)} %pad_maximum_fusion.x_ref, bf16[2,13,16,256]{3,2,1,0:T(8,128)(2,1)S(1)} %pad_maximum_fusion.4.c_ref, bf16[27,128,128]{2,1,0:T(8,128)(2,1)S(1)} %copy-done, ...), custom_call_target="tpu_custom_call" | custom-call | tf_op jit(solution)/shard_map/pallas_call | solution.py:334
  34.1 28.4 %shard_map.71 = (f32[1,432,128]{2,1,0:T(8,128)S(1)}, f32[1,432,128]{2,1,0:T(8,128)S(1)}) custom-call(bf16[8,432,128]{2,1,0:T(8,128)(2,1)S(1)} %bitcast.117, bf16[8,432,128]{2,1,0:T(8,128)(2,1)S(1)} %bitcast.118), custom_call_target="tpu_custom_call" | custom-call | tf_op jit(solution)/shard_map/pallas_call | solution.py:313
  62.6 0.6 pad_maximum_fusion.8.ys_ref
  63.2 0.4 copy.42
  63.7 0.6 pad_maximum_fusion.9.xs_ref
  64.3 9.3 %shard_map.69 = bf16[8,32,512]{2,1,0:T(8,128)(2,1)} custom-call(bf16[2,32,512]{2,1,0:T(8,128)(2,1)} %pad_maximum_fusion.8.ys_ref, bf16[2,32,512]{2,1,0:T(8,128)(2,1)} %pad_maximum_fusion.9.xs_ref), custom_call_target="tpu_custom_call" | custom-call | tf_op jit(solution)/shard_map/pallas_call | solution.py:46
  73.6 0.9 %fusion.23 = (bf16[1,32,512]{2,1,0:T(8,128)(2,1)S(1)}, bf16[1,32,512]{2,1,0:T(8,128)(2,1)S(1)}, bf16[1,32,512]{2,1,0:T(8,128)(2,1)S(1)}, bf16[1,32,512]{2,1,0:T(...) fusion(bf16[8,32,512]{2,1,0:T(8,128)(2,1)} %shard_map.69, ...), kind=kLoop, calls=%fused_computation.80 | loop fusion | flops 32768 | bytes 524290 | tf_op jit(solution)/shard_map/slice | solution.py:60
  75.0 0.2 maximum_bitcast_fusion.2
  75.4 0.2 pad_maximum_fusion.1.x_ref
  75.7 3.2 %shard_map.70 = bf16[2,24,16,512]{3,2,1,0:T(8,128)(2,1)S(1)} custom-call(bf16[4,26,16,512]{3,2,1,0:T(8,128)(2,1)S(1)} %pad_maximum_fusion.1.x_ref, bf16[27,128,128]{2,1,0:T(8,128)(2,1)S(1)} %copy-done), custom_call_target="tpu_custom_call" | custom-call | tf_op jit(solution)/shard_map/pallas_call | solution.py:350
  78.8 0.4 copy.46
  79.3 1.1 %reshape.131 = bf16[1,32,24,4,128]{4,3,2,1,0:T(4,128)(2,1)} reshape(bf16[16,2,24,512]{3,2,1,0:T(8,128)(2,1)S(1)} %copy.46) | data formatting | bytes 1572864 | tf_op jit(solution)/shard_map/reshape | solution.py:358
  80.3 0.7 copy.60
  81.0 0.7 copy.61
  (58 shorter events, 1.9 us)
Async XLA Ops:
  21.0 1.5 %copy-start = (bf16[27,128,128]{2,1,0:T(8,128)(2,1)S(1)}, bf16[27,128,128]{2,1,0:T(8,128)(2,1)}, u32[]{:S(2)}) copy-start(bf16[27,128,128]{2,1,0:T(8,128)(2,1)} %w_ref.1) | copy-start | bytes 2654212
  21.0 2.0 %copy-start.1 = (bf16[27,128,128]{2,1,0:T(8,128)(2,1)S(1)}, bf16[27,128,128]{2,1,0:T(8,128)(2,1)}, u32[]{:S(2)}) copy-start(bf16[27,128,128]{2,1,0:T(8,128)(2,1)} %w2_ref.1) | copy-start | bytes 2654212

commit v4 on v3

--- a/solution.py
+++ b/solution.py
@@ -51,6 +51,10 @@
         scratch_shapes=[pltpu.SemaphoreType.DMA((8,)), pltpu.SemaphoreType.DMA((8,))],
         compiler_params=pltpu.CompilerParams(collective_id=place, has_side_effects=True),
     )(ys, xs)
+    return masked(land)
+
+
+def masked(land):
     out = {}
     x, y = lax.axis_index("gx"), lax.axis_index("gy")
     has_x = {0: True, 1: x > 0, -1: x < lax.axis_size("gx") - 1}
@@ -104,11 +108,6 @@
     column = jnp.concatenate([tail(-1, 0, nj), tail(-1, -1, 1)], 0)[:, None]
     following = jnp.concatenate([long[:, 1:], column], 1)
     return widened(cells, got), jnp.stack([long, following])
-
-
-def widened_again(cells):
-    ys, xs = edges(cells)
-    return widened(cells, swap(jnp.stack(ys), jnp.stack(xs), 2))
 
 
 def conv_dot(x_ref, w_ref, bands, px, half, transposed):
@@ -246,10 +245,10 @@
     return parts.reshape(gx * gy, taps * share, c)
 
 
-def reduce_kernel(orders, dps, first_ref, second_ref, out1_ref, out2_ref, *scratch):
+def reduce_kernel(orders, dps, first_ref, second_ref, ys_ref, xs_ref, out1_ref, out2_ref, land_ref, *scratch):
     steps = len(orders[0]) + len(dps)
     lands, sums = scratch[:steps], scratch[steps : 2 * steps - 1]
-    send_sem, recv_sem = scratch[-2:]
+    send_sem, recv_sem, edge_send, edge_recv = scratch[-4:]
     outs = (out1_ref, out2_ref)
 
     def side(axis, bit):
@@ -262,7 +261,24 @@
         pl.semaphore_signal(
             barrier, inc=1, device_id=side(axis, bit)[1], device_id_type=pl.DeviceIdType.MESH
         )
-    pl.semaphore_wait(barrier, steps)
+    gx, gy = lax.axis_size("gx"), lax.axis_size("gy")
+    x, y = lax.axis_index("gx"), lax.axis_index("gy")
+    partners = [{"gx": (x + dx + gx) % gx, "gy": (y + dy + gy) % gy} for dx, dy in TURNS]
+    for partner in partners:
+        pl.semaphore_signal(barrier, inc=1, device_id=partner, device_id_type=pl.DeviceIdType.MESH)
+    pl.semaphore_wait(barrier, steps + len(TURNS))
+    edge_copies = []
+    for k, (dx, dy) in enumerate(TURNS):
+        copy = pltpu.make_async_remote_copy(
+            src_ref=ys_ref.at[(1 + dy) // 2] if dx == 0 else xs_ref.at[(1 + dx) // 2],
+            dst_ref=land_ref.at[k],
+            send_sem=edge_send.at[k],
+            recv_sem=edge_recv.at[k],
+            device_id=partners[k],
+            device_id_type=pl.DeviceIdType.MESH,
+        )
+        copy.start()
+        edge_copies.append(copy)
 
     held = [first_ref, second_ref]
     halving = len(orders[0])
@@ -299,9 +315,11 @@
             lax.fori_loop(0, size, add, 0)
             following.append(target)
         held = following
-
-
-def reduce_grads(first, second):
+    for copy in edge_copies:
+        copy.wait()
+
+
+def reduce_grads(first, second, ys, xs):
     gx, gy, dp = (lax.axis_size(a) for a in ("gx", "gy", "dp"))
     orders = plane_orders(gx, gy)
     dps = [("dp", 1 << k) for k in range(dp.bit_length() - 1)]
@@ -310,19 +328,20 @@
     rows = taps * share
     sizes = [gx * gy >> (k + 1) for k in range(len(orders[0]))] + [1] * len(dps)
     out = jax.ShapeDtypeStruct((1, rows, c), F32)
-    one, two = pl.pallas_call(
+    one, two, land = pl.pallas_call(
         functools.partial(reduce_kernel, orders, dps),
-        out_shape=(out, out),
-        in_specs=[VMEM] * 2,
-        out_specs=(VMEM,) * 2,
+        out_shape=(out, out, jax.ShapeDtypeStruct((8,) + ys.shape[1:], BF)),
+        in_specs=[VMEM] * 4,
+        out_specs=(VMEM,) * 3,
         scratch_shapes=[pltpu.VMEM((2, n, rows, c), BF) for n in sizes]
         + [pltpu.VMEM((2, n, rows, c), BF) for n in sizes[:-1]]
-        + [pltpu.SemaphoreType.DMA((len(sizes), 2)), pltpu.SemaphoreType.DMA((len(sizes), 2))],
+        + [pltpu.SemaphoreType.DMA((len(sizes), 2)), pltpu.SemaphoreType.DMA((len(sizes), 2))]
+        + [pltpu.SemaphoreType.DMA((8,)), pltpu.SemaphoreType.DMA((8,))],
         compiler_params=pltpu.CompilerParams(
             collective_id=0, has_side_effects=True, vmem_limit_bytes=48 * 1024 * 1024
         ),
-    )(by_halves(first, orders[0], gx, gy), by_halves(second, orders[1], gx, gy))
-    return one.reshape(taps, share, c), two.reshape(taps, share, c)
+    )(by_halves(first, orders[0], gx, gy), by_halves(second, orders[1], gx, gy), ys, xs)
+    return one.reshape(taps, share, c), two.reshape(taps, share, c), masked(land)
 
 
 def local(volume, cotangent, w_first, w_second):
@@ -346,7 +365,8 @@
         ],
         compiler_params=PARAMS,
     )(cells, grads, w_first, w_second)
-    share = reduce_grads(first, second)
+    ys, xs = edges(grad_pre)
+    *share, got = reduce_grads(first, second, jnp.stack(ys), jnp.stack(xs))
     out = pl.pallas_call(
         volume_kernel,
         out_shape=jax.ShapeDtypeStruct((2, ny, nm, lanes), BF),
@@ -354,7 +374,7 @@
         out_specs=VMEM,
         scratch_shapes=[pltpu.VMEM((2, 2 * c, 27 * c), BF)],
         compiler_params=PARAMS,
-    )(widened_again(grad_pre), w_first)
+    )(widened(grad_pre, got), w_first)
     grad_volume = out.transpose(2, 0, 1, 3).reshape(1, nx, ny, nz, c)
     return (grad_volume, share[0], share[1])
 

time: 82.1 us -> 73.3 us (0.89)
  Pallas kernels: 65.2 us -> 58.5 us
  other arithmetic: 7.33 us -> 5.19 us
    pallas_call x2 -> x1, Pallas kernels: 22.8 us -> 13.6 us  [swap(): pl.pallas_call(swap_kernel, out_shape=jax.ShapeDtypeStruct((8,) + ys.shap...]
    pallas_call x1, Pallas kernels: 28.4 us -> 31.1 us  [reduce_grads(): pl.pallas_call(functools.partial(reduce_kernel, orders, dps), out_shape=(...]
    another operation x2, other arithmetic: 1.28 us -> 0.02 us  [local(): *share, got = reduce_grads(first, second, jnp.stack(ys), jnp.stack(xs))]
    slice x2, other arithmetic: 1.9 us -> 1.03 us  [masked(): out[dx, dy] = jnp.where(good, land[k], jnp.zeros((), BF))]
where the time goes in v4:
time: 73.3 us; the launch traced here: 72.9 us
  Pallas kernels  58.5 us (80%)
  local copies, waits for them, and re-layouts  8.01 us (11%)
  other arithmetic  5.19 us (7%)
  between operations  1.18 us (2%)
    pallas_call x1, Pallas kernels, reduce_grads(): pl.pallas_call(functools.partial(reduce_kernel, orders, dps), out_shape=(...  31.1 us
    pallas_call x1, Pallas kernels, swap(): pl.pallas_call(swap_kernel, out_shape=jax.ShapeDtypeStruct((8,) + ys.shap...  13.6 us
    pallas_call x1, Pallas kernels, local(): pl.pallas_call(grads_kernel, out_shape=(jax.ShapeDtypeStruct((2, ny, nm,...  10.8 us
    pallas_call x1, Pallas kernels, local(): pl.pallas_call(volume_kernel, out_shape=jax.ShapeDtypeStruct((2, ny, nm,...  3.15 us
    unnamed x9, local copies, waits for them, and re-layouts  2.93 us
    another operation x6, other arithmetic, widened(): return jnp.stack([before, even, odd, after])  2.3 us
    reshape x2, local copies, waits for them, and re-layouts, local(): split = volume.reshape(nm, 2, ny, lanes).transpose(1, 2, 0, 3)  2.09 us

profile of v4, /device:TPU:0, one launch (start us, length us, event | category | flops | bytes accessed | tf_op | source)
XLA Modules:
  0.0 72.9 jit_solution(16002583993107342314)
XLA Ops:
  0.7 1.0 %copy.36 = bf16[1,16,12,2,128]{4,3,1,2,0:T(2,128)(2,1)S(1)} copy(bf16[1,16,12,2,128]{4,3,2,1,0:T(2,128)(2,1)} %param.5) | data formatting | bytes 196608 | tf_op args[1]
  1.7 1.7 %reshape.127 = bf16[16,2,24,512]{3,2,1,0:T(8,128)(2,1)S(1)} reshape(bf16[1,32,24,4,128]{4,3,2,1,0:T(4,128)(2,1)} %param.4) | data formatting | bytes 1572864 | tf_op jit(solution)/shard_map/reshape | solution.py:350
  3.4 0.4 copy.56
  3.9 0.7 pad_maximum_fusion.6.ys_ref
  4.7 0.7 pad_maximum_fusion.7.xs_ref
  5.3 13.6 %shard_map.67 = bf16[8,48,512]{2,1,0:T(8,128)(2,1)} custom-call(bf16[2,48,512]{2,1,0:T(8,128)(2,1)} %pad_maximum_fusion.6.ys_ref, bf16[2,48,512]{2,1,0:T(8,128)(2,1)} %pad_maximum_fusion.7.xs_ref), custom_call_target="tpu_custom_call" | custom-call | tf_op jit(solution)/shard_map/pallas_call | solution.py:46
  18.9 1.0 %fusion.22 = (bf16[1,48,512]{2,1,0:T(8,128)(2,1)S(1)}, bf16[1,48,512]{2,1,0:T(8,128)(2,1)S(1)}, bf16[1,48,512]{2,1,0:T(8,128)(2,1)S(1)}, bf16[1,48,512]{2,1,0:T(...) fusion(bf16[8,48,512]{2,1,0:T(8,128)(2,1)} %shard_map.67, ...), kind=kLoop, calls=%fused_computation.79 | loop fusion | flops 73728 | bytes 786435 | tf_op jit(solution)/shard_map/slice | solution.py:64
  20.5 0.2 maximum_bitcast_fusion
  20.7 0.1 slice.274
  20.9 0.1 maximum_bitcast_fusion.1
  21.0 1.5 %pad_maximum_fusion.x_ref = bf16[4,26,16,512]{3,2,1,0:T(8,128)(2,1)} fusion(bf16[1,26,16,512]{3,2,1,0:T(8,128)(2,1)S(1)} %maximum_bitcast_fusion.1, bf16[2,1,16,512]{3,2,1,0:T(8,128)(2,1)S(1)} %bitcast.141, bf16[2,24,16,512]{3,2,1,0:T(8,128)(2,1)S(1)} %bitcast.127, bf16[2,1,16,512]{3,2,1,0:T(8,128)(2,1)S(1)} %bitcast.139, ...), kind=kLoop, calls=%fused_computation | loop fusion | flops 3407872 | bytes 3407872 | tf_op jit(solution)/shard_map/stack | solution.py:92
  22.5 0.6 copy-done.1
  23.0 10.8 %shard_map.68 = (bf16[2,24,16,512]{3,2,1,0:T(8,128)(2,1)S(1)}, bf16[27,128,128]{2,1,0:T(8,128)(2,1)S(1)}, bf16[27,128,128]{2,1,0:T(8,128)(2,1)S(1)}) custom-call(bf16[4,26,16,512]{3,2,1,0:T(8,128)(2,1)} %pad_maximum_fusion.x_ref, bf16[2,13,16,256]{3,2,1,0:T(8,128)(2,1)S(1)} %pad_maximum_fusion.4.c_ref, bf16[27,128,128]{2,1,0:T(8,128)(2,1)S(1)} %copy-done, ...), custom_call_target="tpu_custom_call" | custom-call | tf_op jit(solution)/shard_map/pallas_call | solution.py:353
  33.8 0.2 copy.42
  34.0 0.2 copy.43
  34.2 0.4 copy.44
  34.7 31.1 %shard_map.69 = (f32[1,432,128]{2,1,0:T(8,128)S(1)}, f32[1,432,128]{2,1,0:T(8,128)S(1)}, bf16[8,32,512]{2,1,0:T(8,128)(2,1)S(1)}) custom-call(bf16[8,432,128]{2,1,0:T(8,128)(2,1)S(1)} %bitcast.117, bf16[8,432,128]{2,1,0:T(8,128)(2,1)S(1)} %bitcast.118, bf16[2,32,512]{2,1,0:T(8,128)(2,1)S(1)} %pad_maximum_fusion.8.ys_ref, ...), custom_call_target="tpu_custom_call" | custom-call | tf_op jit(solution)/shard_map/pallas_call | solution.py:331
  66.2 0.2 maximum_bitcast_fusion.2
  66.6 0.2 pad_maximum_fusion.1.x_ref
  66.9 3.1 %shard_map.70 = bf16[2,24,16,512]{3,2,1,0:T(8,128)(2,1)S(1)} custom-call(bf16[4,26,16,512]{3,2,1,0:T(8,128)(2,1)S(1)} %pad_maximum_fusion.1.x_ref, bf16[27,128,128]{2,1,0:T(8,128)(2,1)S(1)} %copy-done), custom_call_target="tpu_custom_call" | custom-call | tf_op jit(solution)/shard_map/pallas_call | solution.py:370
  70.1 0.4 copy.48
  70.5 1.1 %reshape.135 = bf16[1,32,24,4,128]{4,3,2,1,0:T(4,128)(2,1)} reshape(bf16[16,2,24,512]{3,2,1,0:T(8,128)(2,1)S(1)} %copy.48) | data formatting | bytes 1572864 | tf_op jit(solution)/shard_map/reshape | solution.py:378
  71.6 0.7 copy.60
  72.2 0.7 copy.61
  (57 shorter events, 1.4 us)
Async XLA Ops:
  21.0 1.5 %copy-start = (bf16[27,128,128]{2,1,0:T(8,128)(2,1)S(1)}, bf16[27,128,128]{2,1,0:T(8,128)(2,1)}, u32[]{:S(2)}) copy-start(bf16[27,128,128]{2,1,0:T(8,128)(2,1)} %w_ref.1) | copy-start | bytes 2654212
  21.0 2.0 %copy-start.1 = (bf16[27,128,128]{2,1,0:T(8,128)(2,1)S(1)}, bf16[27,128,128]{2,1,0:T(8,128)(2,1)}, u32[]{:S(2)}) copy-start(bf16[27,128,128]{2,1,0:T(8,128)(2,1)} %w2_ref.1) | copy-start | bytes 2654212
